TPU v7x, 256 devices: a whole 4x4x8 slice. The times are simulated.
256 devices in a mesh: gx: 4 (over y), gy: 8 (over z), gz: 8 (over x, core).
Axes of the slice: x: 4, y: 4, z: 8, core: 2. Of those that a mesh axis runs over, the one named last changes fastest.
Arguments:
- seg_state: float32 [4, 8, 8, 32, 9, 128], P('gx', 'gy', 'gz'), as said below
- seg_cells: int32 [4, 8, 8, 32, 128], P('gx', 'gy', 'gz'), may hold values from 0 to 15
- seg_nodes: int32 [4, 8, 8, 2, 4096], P('gx', 'gy', 'gz'), may hold values from 0 to 4095, each once within a row
- pair_blocks: int32 [4, 8, 8, 2, 128], P('gx', 'gy', 'gz'), may hold values from 0 to 31
- pair_offsets: int32 [4, 8, 8, 128], P('gx', 'gy', 'gz'), may hold values from 0 to 26
- pair_count: int32 [4, 8, 8], P('gx', 'gy', 'gz'), may hold values from 64 to 128, as said below
Outputs:
- node_velocity: float32 [4, 8, 8, 3, 4096], P('gx', 'gy', 'gz')
Inputs may be any that keep to these rules, and one draw needn't show every extreme that they name: `seg_state`: rows 0 to 2 of the component dimension lie in [0, 1). `pair_count`: some domain has all 128 slots live, another exactly half of them.
All inputs are finite; a program needn't handle non-finite values.
Results may differ from a plain program's by a relative error of at most 0.0003.
Values sent between devices are 32-bit elements; how exact they have to be, the bound alone decides.
A program may use at most 64 MiB of HBM per device.

v0:
```python
import jax
import jax.numpy as jnp
from jax import lax
from jax.sharding import PartitionSpec as P

CELLS = 16


PAIR_STRENGTH = 0.1
CORE_SQUARED = 0.2
FAR_STRENGTH = 0.008
DRAG_FLOOR = 0.5


def extended(block, sides, width):
    for axis, dim in sides:
        count = lax.axis_size(axis)
        forward = [(i, i + 1) for i in range(count - 1)]
        forward.append((count - 1, 0))
        backward = [(target, source) for source, target in forward]
        low = lax.ppermute(
            lax.slice_in_dim(block, block.shape[dim] - width, None, axis=dim), axis, forward
        )
        high = lax.ppermute(lax.slice_in_dim(block, 0, width, axis=dim), axis, backward)
        block = jnp.concatenate([low, block, high], axis=dim)
    return block


def outer_dot(first_vec, second_vec):
    return (
        first_vec[0][:, None] * second_vec[0][None, :]
        + first_vec[1][:, None] * second_vec[1][None, :]
        + first_vec[2][:, None] * second_vec[2][None, :]
    )


def tile_force(own_tile, other_tile, shift):
    own_pos = own_tile[0:3]
    own_line = own_tile[3:6]
    own_burgers = own_tile[6:9]
    other_pos = other_tile[0:3] + shift[:, None]
    other_line = other_tile[3:6]
    other_burgers = other_tile[6:9]
    separation = own_pos[:, :, None] - other_pos[:, None, :]
    radius_sq = (
        separation[0] * separation[0]
        + separation[1] * separation[1]
        + separation[2] * separation[2]
        + CORE_SQUARED
    )
    inverse = lax.rsqrt(radius_sq)
    inv_cube = inverse * inverse * inverse
    inv_fifth = inv_cube * inverse * inverse
    coupling = outer_dot(own_burgers, other_burgers) * outer_dot(own_line, other_line)
    crossed = outer_dot(own_burgers, other_line) * outer_dot(own_line, other_burgers)
    strength = PAIR_STRENGTH * (coupling * inv_cube + CORE_SQUARED * crossed * inv_fifth)
    weighted = strength[None] * separation
    return (jnp.sum(weighted, axis=2), -jnp.sum(weighted, axis=1))


def cell_coords(flat_ids, grid_x, grid_y, grid_z):
    span_x = CELLS // grid_x
    span_y = CELLS // grid_y
    span_z = CELLS // grid_z
    per_domain = span_x * span_y * span_z
    owner = flat_ids // per_domain
    local_ids = flat_ids % per_domain
    owner_x = owner // (grid_y * grid_z)
    owner_y = owner // grid_z % grid_y
    owner_z = owner % grid_z
    inner_x = local_ids // (span_y * span_z)
    inner_y = local_ids // span_z % span_y
    inner_z = local_ids % span_z
    return (owner_x * span_x + inner_x, owner_y * span_y + inner_y, owner_z * span_z + inner_z)


def far_kernel(targets, grid_x, grid_y, grid_z):
    every_cell = jnp.arange(CELLS**3, dtype=jnp.int32)
    source = cell_coords(every_cell, grid_x, grid_y, grid_z)
    target = cell_coords(targets, grid_x, grid_y, grid_z)
    half = CELLS // 2
    deltas = [(source[k][:, None] - target[k][None, :] + half) % CELLS - half for k in range(3)]
    largest = jnp.maximum(jnp.maximum(jnp.abs(deltas[0]), jnp.abs(deltas[1])), jnp.abs(deltas[2]))
    dist_sq = (deltas[0] * deltas[0] + deltas[1] * deltas[1] + deltas[2] * deltas[2]).astype(
        jnp.float32
    )
    return jnp.where(
        largest > 1, FAR_STRENGTH * lax.rsqrt(jnp.maximum(dist_sq, 1.0)), jnp.float32(0.0)
    )


def layout(blocks):
    return jnp.transpose(blocks, (1, 0, 2)).reshape(blocks.shape[1], -1)


def moment_terms(line, burgers, cell_hot):
    products = (burgers[:, None, :] * line[None, :, :]).reshape(9, -1)
    return jnp.dot(products, cell_hot, precision=lax.Precision.HIGHEST)


def segment_far(local_field, cell_hot, line, burgers):
    per_seg = jnp.dot(local_field, cell_hot.T, precision=lax.Precision.HIGHEST)
    pulled = [
        per_seg[3 * k] * burgers[0]
        + per_seg[3 * k + 1] * burgers[1]
        + per_seg[3 * k + 2] * burgers[2]
        for k in range(3)
    ]
    return jnp.stack(
        [
            pulled[1] * line[2] - pulled[2] * line[1],
            pulled[2] * line[0] - pulled[0] * line[2],
            pulled[0] * line[1] - pulled[1] * line[0],
        ]
    )


def node_velocity_of(seg_force, line, nodes):
    seg_total = seg_force.shape[1]
    length = jnp.sqrt(line[0] * line[0] + line[1] * line[1] + line[2] * line[2])
    halves = 0.5 * jnp.concatenate([seg_force, length[None]], axis=0)
    block_rows = 512
    node_ids = jnp.arange(seg_total, dtype=jnp.int32)

    def add_block(turn_index, totals):
        first_slot = turn_index * block_rows
        part_rows = lax.dynamic_slice_in_dim(halves, first_slot, block_rows, 1)
        ends = lax.dynamic_slice_in_dim(nodes, first_slot, block_rows, 1)
        node_hot = (ends[0][:, None] == node_ids[None, :]).astype(jnp.float32) + (
            ends[1][:, None] == node_ids[None, :]
        ).astype(jnp.float32)
        return totals + jnp.dot(part_rows, node_hot, precision=lax.Precision.HIGHEST)

    totals = lax.fori_loop(
        0, seg_total // block_rows, add_block, jnp.zeros((4, seg_total), jnp.float32)
    )
    return totals[:3] / jnp.maximum(totals[3], DRAG_FLOOR)


def code_shifts(code_group):
    return jnp.stack(
        [code_group // 9 - 1, code_group // 3 % 3 - 1, code_group % 3 - 1], axis=1
    ).astype(jnp.float32)


def shards(seg_state, seg_cells, seg_nodes, pair_blocks, pair_offsets, pair_count):
    grid_x = lax.axis_size("gx")
    grid_y = lax.axis_size("gy")
    grid_z = lax.axis_size("gz")
    blocks = seg_state.shape[3]
    width = seg_state.shape[5]
    own_blocks = seg_state[0, 0, 0]
    ghosts = extended(seg_state, (("gx", 0), ("gy", 1), ("gz", 2)), 1)
    ghosts = ghosts.reshape(27 * blocks, 9, width)
    slots = pair_offsets.shape[3]
    group_size = min(16, slots)
    first_blocks = pair_blocks[0, 0, 0, 0]
    second_blocks = pair_blocks[0, 0, 0, 1]
    codes = pair_offsets[0, 0, 0]
    live_count = pair_count[0, 0, 0]
    block_ids = jnp.arange(blocks, dtype=jnp.int32)
    ghost_ids = jnp.arange(27 * blocks, dtype=jnp.int32)
    group_ids = jnp.arange(group_size, dtype=jnp.int32)
    turn_count = (live_count + group_size - 1) // group_size

    def tile_group(turn_index, totals):
        first_slot = turn_index * group_size
        first = lax.dynamic_slice_in_dim(first_blocks, first_slot, group_size)
        second = lax.dynamic_slice_in_dim(second_blocks, first_slot, group_size)
        code_group = lax.dynamic_slice_in_dim(codes, first_slot, group_size)
        live_mask = (first_slot + group_ids < live_count).astype(jnp.float32)
        target = code_group * blocks + second
        own_tiles = jnp.take(own_blocks, first, axis=0)
        other_tiles = jnp.take(ghosts, target, axis=0)
        on_own, on_peer = jax.vmap(tile_force)(own_tiles, other_tiles, code_shifts(code_group))
        own_hot = (first[:, None] == block_ids[None, :]).astype(jnp.float32) * live_mask[:, None]
        own_sum = totals[0] + jnp.einsum(
            "gb,gkn->bkn", own_hot, on_own, precision=lax.Precision.HIGHEST
        )
        react_hot = (target[:, None] == ghost_ids[None, :]).astype(jnp.float32) * live_mask[:, None]
        react_sum = totals[1] + jnp.einsum(
            "gb,gkn->bkn", react_hot, on_peer, precision=lax.Precision.HIGHEST
        )
        return (own_sum, react_sum)

    own_init = jnp.zeros((blocks, 3, width), jnp.float32)
    own_sum, react_sum = lax.fori_loop(
        0, turn_count, tile_group, (own_init, jnp.zeros((27 * blocks, 3, width), jnp.float32))
    )
    react_grid = react_sum.reshape(3, 3, 3, blocks, 3, width)
    padded = extended(react_grid, (("gx", 0), ("gy", 1), ("gz", 2)), 1)
    returned = jnp.sum(padded[0::2, 0::2, 0::2], axis=(0, 1, 2))
    near_force = layout(own_sum + returned)
    columns = layout(own_blocks)
    cell_dev = CELLS**3 // (grid_x * grid_y * grid_z)
    cell_ids = jnp.arange(cell_dev, dtype=jnp.int32)
    seg_cell_ids = seg_cells[0, 0, 0].reshape(-1)
    cell_hot = (seg_cell_ids[:, None] == cell_ids[None, :]).astype(jnp.float32)
    moments = moment_terms(columns[3:6], columns[6:9], cell_hot)
    domain = (lax.axis_index("gx") * grid_y + lax.axis_index("gy")) * grid_z + lax.axis_index("gz")
    placed = lax.dynamic_update_slice(
        jnp.zeros((9, CELLS**3), jnp.float32), moments, (jnp.int32(0), domain * cell_dev)
    )
    all_moments = lax.psum(placed, ("gx", "gy", "gz"))
    targets = domain * cell_dev + cell_ids
    kernel = far_kernel(targets, grid_x, grid_y, grid_z)
    local_field = jnp.dot(all_moments, kernel, precision=lax.Precision.HIGHEST)
    seg_force = near_force + segment_far(local_field, cell_hot, columns[3:6], columns[6:9])
    velocity = node_velocity_of(seg_force, columns[3:6], seg_nodes[0, 0, 0])
    return velocity[None, None, None]


def solution(mesh):
    placed = (
        P("gx", "gy", "gz", None, None, None),
        P("gx", "gy", "gz", None, None),
        P("gx", "gy", "gz", None, None),
        P("gx", "gy", "gz", None, None),
        P("gx", "gy", "gz", None),
        P("gx", "gy", "gz"),
    )
    return jax.shard_map(
        shards,
        mesh=mesh,
        in_specs=placed,
        out_specs=P("gx", "gy", "gz", None, None),
        check_vma=False,
    )
```

profile of v0, /device:TPU:1, one launch (start us, length us, event | category | flops | bytes accessed | tf_op | source)
XLA Modules:
  0.0 385.7 jit_solution(5175657654649566171)
XLA Ops:
  6.5 2.1 collective-permute-start
  13.8 2.5 collective-permute-start.2
  16.3 4.0 %collective-permute-start.3 = (f32[3,1,1,32,9,128]{5,3,4,2,1,0:T(8,128)S(1)}, f32[3,1,1,32,9,128]{5,3,4,2,1,0:T(8,128)S(1)}, u32[]{:S(2)}, u32[]{:S(2)}) collective-permute-start(f32[3,1,1,32,9,128]{5,3,4,2,1,0:T(8,128)S(1)} %constant_dynamic-update-slice_fusion), channel_id=1, source_target_pairs={{8,0},{16,8},{24,16},{32,24},{40,32},{48,40},{56,48},{0,56},{9,1},... | collective-permute-start | bytes 1327112 | tf_op jit(solution)/shard_map/ppermute | solution.py:24
  20.4 8.9 %collective-permute-done.2 = f32[3,1,1,32,9,128]{5,3,4,2,1,0:T(8,128)S(1)} collective-permute-done((f32[3,1,1,32,9,128]{5,3,4,2,1,0:T(8,128)S(1)}, f32[3,1,1,32,9,128]{5,3,4,2,1,0:T(8,128)S(1)}, u32[]{:S(2)}, u32[]{:S(2)}) %collective-permute-start.2) | collective-permute-done | bytes 442400 | tf_op jit(solution)/shard_map/ppermute | solution.py:21
  29.4 3.2 collective-permute-start.4
  35.0 12.4 %collective-permute-done.4 = f32[3,3,1,32,9,128]{5,3,4,2,1,0:T(8,128)} collective-permute-done((f32[3,3,1,32,9,128]{5,3,4,2,1,0:T(8,128)S(1)}, f32[3,3,1,32,9,128]{5,3,4,2,1,0:T(8,128)}, u32[]{:S(2)}, u32[]{:S(2)}) %collective-permute-start.4) | collective-permute-done | bytes 1327136 | tf_op jit(solution)/shard_map/ppermute | solution.py:21
  47.4 2.9 collective-permute-done.5
  50.3 2.2 pad_maximum_fusion.1
  52.5 6.4 %copy.30 = f32[3,3,3,32,9,128]{5,4,3,2,1,0:T(8,128)} copy(f32[3,3,3,32,9,128]{5,3,4,2,1,0:T(8,128)S(1)} %pad_maximum_fusion.1) | data formatting | bytes 7962624 | tf_op jit(solution)/shard_map/concatenate | solution.py:25
  59.0 75.9 %while.31 = (s32[]{:T(128)}, f32[32,3,128]{2,0,1:T(8,128)S(1)}, f32[864,3,128]{2,0,1:T(8,128)S(1)}, s32[]{:T(128)}, s32[128]{0:T(128)S(1)}, /*index=5*/s32[]{:T(...) while((s32[]{:T(128)}, f32[32,3,128]{2,0,1:T(8,128)S(1)}, ...), condition=%wide.region_3.4_spmd.clone, body=%wide.region_0.3_spmd.clone.sunk | while | flops 80104376 | bytes 12331587 | solution.py:187
  59.5 3.6 gather_fusion
  65.0 2.1 fusion.167
  67.1 2.0 multiply_reduce_fusion.3
  69.7 1.8 convolution_add_fusion.5
  72.1 3.6 gather_fusion
  77.6 2.1 fusion.167
  79.7 2.0 multiply_reduce_fusion.3
  82.3 1.8 convolution_add_fusion.5
  84.8 3.6 gather_fusion
  90.2 2.1 fusion.167
  92.3 2.0 multiply_reduce_fusion.3
  95.0 1.8 convolution_add_fusion.5
  97.4 3.6 gather_fusion
  102.8 2.1 fusion.167
  104.9 2.0 multiply_reduce_fusion.3
  110.0 3.6 gather_fusion
  115.5 2.1 fusion.167
  117.5 2.0 multiply_reduce_fusion.3
  122.6 3.6 gather_fusion
  128.0 2.1 fusion.167
  130.1 2.0 multiply_reduce_fusion.3
  135.7 25.2 %collective-permute-start.6 = (f32[1,3,3,32,3,128]{5,3,2,1,0,4:T(8,128)}, f32[1,3,3,32,3,128]{5,3,2,1,0,4:T(8,128)S(1)}, u32[]{:S(2)}, u32[]{:S(2)}) collective-permute-start(f32[1,3,3,32,3,128]{5,3,2,1,0,4:T(8,128)} %bitcast.7), channel_id=1, source_target_pairs={{0,64},{64,128},{128,192},{192,0},{1,65},{65,129},{129,193},{193,1... | collective-permute-start | bytes 1327112 | tf_op jit(solution)/shard_map/ppermute | solution.py:21
  160.9 121.4 %all-reduce.2.cloned.1.call-done = f32[9,4096]{1,0:T(8,128)} async-done(((f32[9,4096]{1,0:T(8,128)}), f32[9,4096]{1,0:T(8,128)}) %all-reduce.2.cloned.1.call-update) | async-done | bytes 147472 | tf_op jit(solution)/shard_map/psum | solution.py:204
  282.3 2.0 fusion.51
  286.0 2.2 collective-permute-start.9
  288.3 14.5 %collective-permute-done.8 = f32[5,1,3,32,3,128]{5,3,2,1,0,4:T(8,128)S(1)} collective-permute-done((f32[5,1,3,32,3,128]{5,3,2,1,0,4:T(8,128)S(1)}, f32[5,1,3,32,3,128]{5,3,2,1,0,4:T(8,128)S(1)}, u32[]{:S(2)}, u32[]{:S(2)}) %collective-permute-start.8) | collective-permute-done | bytes 737312 | tf_op jit(solution)/shard_map/ppermute | solution.py:21
  304.6 2.3 collective-permute-start.10
  307.1 13.5 %collective-permute-done.10 = f32[5,5,1,32,3,128]{5,3,2,1,0,4:T(8,128)S(1)} collective-permute-done((f32[5,5,1,32,3,128]{5,3,2,1,0,4:T(8,128)S(1)}, f32[5,5,1,32,3,128]{5,3,2,1,0,4:T(8,128)S(1)}, u32[]{:S(2)}, u32[]{:S(2)}) %collective-permute-start.10) | collective-permute-done | bytes 1228832 | tf_op jit(solution)/shard_map/ppermute | solution.py:21
  320.6 2.5 collective-permute-done.11
  323.9 54.2 %while.32 = (s32[]{:T(128)}, f32[4,4096]{1,0:T(4,128)S(1)}, f32[4,4096]{1,0:T(4,128)S(1)}, s32[2,4096]{1,0:T(2,128)}, s32[]{:T(128)}, /*index=5*/s32[]{:T(128)}, s32[]{:T(128)}, s32[]{:T(128)}, s32[]{}) while((s32[]{:T(128)}, f32[4,4096]{1,0:T(4,128)S(1)}, f32[4,4096]{1,0:T(4,128)S(1)}, s32[2,4096]{1,0:T(2,128)}, ...), condition=%wide.region_7.8_spmd.clone.clone, body=%wide.region_6.7_spmd.clone.clone.sunk | while | flops 111181832 | bytes 151725 | solution.py:134
  324.8 5.9 %fusion.170 = f32[4,4096]{1,0:T(4,128)S(1)} fusion(s32[512]{0:T(512)S(1)} %bitcast.183, s32[512]{0:T(512)S(1)} %bitcast.182, f32[4,4096]{1,0:T(4,128)S(1)} %get-tuple-element.635, pred[]{:T(512)S(6)} %compare.124, f32[4,4096]{1,0:T(4,128)S(1)} %get-tuple-element.645, s32[]{:T(128)S(6)} %select_n.556), kind=kOutput, calls=%fused_computation.69.clone.1 | convolution fusion | flops 111181824 | bytes 143365 | tf_op jit(solution)/shard_map/while/body/eval_jaxpr/dot_general | solution.py:132
  331.6 5.9 %fusion.170 = f32[4,4096]{1,0:T(4,128)S(1)} fusion(s32[512]{0:T(512)S(1)} %bitcast.183, s32[512]{0:T(512)S(1)} %bitcast.182, f32[4,4096]{1,0:T(4,128)S(1)} %get-tuple-element.635, pred[]{:T(512)S(6)} %compare.124, f32[4,4096]{1,0:T(4,128)S(1)} %get-tuple-element.645, s32[]{:T(128)S(6)} %select_n.556), kind=kOutput, calls=%fused_computation.69.clone.1 | convolution fusion | flops 111181824 | bytes 143365 | tf_op jit(solution)/shard_map/while/body/eval_jaxpr/dot_general | solution.py:132
  338.3 5.9 %fusion.170 = f32[4,4096]{1,0:T(4,128)S(1)} fusion(s32[512]{0:T(512)S(1)} %bitcast.183, s32[512]{0:T(512)S(1)} %bitcast.182, f32[4,4096]{1,0:T(4,128)S(1)} %get-tuple-element.635, pred[]{:T(512)S(6)} %compare.124, f32[4,4096]{1,0:T(4,128)S(1)} %get-tuple-element.645, s32[]{:T(128)S(6)} %select_n.556), kind=kOutput, calls=%fused_computation.69.clone.1 | convolution fusion | flops 111181824 | bytes 143365 | tf_op jit(solution)/shard_map/while/body/eval_jaxpr/dot_general | solution.py:132
  345.1 5.9 %fusion.170 = f32[4,4096]{1,0:T(4,128)S(1)} fusion(s32[512]{0:T(512)S(1)} %bitcast.183, s32[512]{0:T(512)S(1)} %bitcast.182, f32[4,4096]{1,0:T(4,128)S(1)} %get-tuple-element.635, pred[]{:T(512)S(6)} %compare.124, f32[4,4096]{1,0:T(4,128)S(1)} %get-tuple-element.645, s32[]{:T(128)S(6)} %select_n.556), kind=kOutput, calls=%fused_computation.69.clone.1 | convolution fusion | flops 111181824 | bytes 143365 | tf_op jit(solution)/shard_map/while/body/eval_jaxpr/dot_general | solution.py:132
  351.9 5.9 %fusion.170 = f32[4,4096]{1,0:T(4,128)S(1)} fusion(s32[512]{0:T(512)S(1)} %bitcast.183, s32[512]{0:T(512)S(1)} %bitcast.182, f32[4,4096]{1,0:T(4,128)S(1)} %get-tuple-element.635, pred[]{:T(512)S(6)} %compare.124, f32[4,4096]{1,0:T(4,128)S(1)} %get-tuple-element.645, s32[]{:T(128)S(6)} %select_n.556), kind=kOutput, calls=%fused_computation.69.clone.1 | convolution fusion | flops 111181824 | bytes 143365 | tf_op jit(solution)/shard_map/while/body/eval_jaxpr/dot_general | solution.py:132
  358.6 5.9 %fusion.170 = f32[4,4096]{1,0:T(4,128)S(1)} fusion(s32[512]{0:T(512)S(1)} %bitcast.183, s32[512]{0:T(512)S(1)} %bitcast.182, f32[4,4096]{1,0:T(4,128)S(1)} %get-tuple-element.635, pred[]{:T(512)S(6)} %compare.124, f32[4,4096]{1,0:T(4,128)S(1)} %get-tuple-element.645, s32[]{:T(128)S(6)} %select_n.556), kind=kOutput, calls=%fused_computation.69.clone.1 | convolution fusion | flops 111181824 | bytes 143365 | tf_op jit(solution)/shard_map/while/body/eval_jaxpr/dot_general | solution.py:132
  365.4 5.9 %fusion.170 = f32[4,4096]{1,0:T(4,128)S(1)} fusion(s32[512]{0:T(512)S(1)} %bitcast.183, s32[512]{0:T(512)S(1)} %bitcast.182, f32[4,4096]{1,0:T(4,128)S(1)} %get-tuple-element.635, pred[]{:T(512)S(6)} %compare.124, f32[4,4096]{1,0:T(4,128)S(1)} %get-tuple-element.645, s32[]{:T(128)S(6)} %select_n.556), kind=kOutput, calls=%fused_computation.69.clone.1 | convolution fusion | flops 111181824 | bytes 143365 | tf_op jit(solution)/shard_map/while/body/eval_jaxpr/dot_general | solution.py:132
  372.2 5.9 %fusion.170 = f32[4,4096]{1,0:T(4,128)S(1)} fusion(s32[512]{0:T(512)S(1)} %bitcast.183, s32[512]{0:T(512)S(1)} %bitcast.182, f32[4,4096]{1,0:T(4,128)S(1)} %get-tuple-element.635, pred[]{:T(512)S(6)} %compare.124, f32[4,4096]{1,0:T(4,128)S(1)} %get-tuple-element.645, s32[]{:T(128)S(6)} %select_n.556), kind=kOutput, calls=%fused_computation.69.clone.1 | convolution fusion | flops 111181824 | bytes 143365 | tf_op jit(solution)/shard_map/while/body/eval_jaxpr/dot_general | solution.py:132
  (174 shorter events, 43.5 us)
Async XLA Ops:
  6.5 275.8 %all-reduce.2.cloned.1.call-start = ((), (), s32[]{:S(2)}) async-start(), calls=%async_computation | async-start | bytes 524288 | tf_op jit(solution)/shard_map/psum | solution.py:204
  6.5 6.3 %collective-permute-start = (f32[1,1,1,32,9,128]{5,3,4,2,1,0:T(8,128)}, f32[1,1,1,32,9,128]{5,3,4,2,1,0:T(8,128)S(1)}, u32[]{:S(2)}, u32[]{:S(2)}) collective-permute-start(f32[1,1,1,32,9,128]{5,3,4,2,1,0:T(8,128)} %param.10), channel_id=1, source_target_pairs={{0,64},{64,128},{128,192},{192,0},{1,65},{65,129},{129,193},{193,1... | collective-permute-start | bytes 442376 | tf_op jit(solution)/shard_map/ppermute | solution.py:21
  8.7 5.1 %collective-permute-start.1 = (f32[1,1,1,32,9,128]{5,3,4,2,1,0:T(8,128)}, f32[1,1,1,32,9,128]{5,3,4,2,1,0:T(8,128)S(1)}, u32[]{:S(2)}, u32[]{:S(2)}) collective-permute-start(f32[1,1,1,32,9,128]{5,3,4,2,1,0:T(8,128)} %param.10), channel_id=1, source_target_pairs={{64,0},{128,64},{192,128},{0,192},{65,1},{129,65},{193,129},{1,193... | collective-permute-start | bytes 442376 | tf_op jit(solution)/shard_map/ppermute | solution.py:24
  12.9 19.9 %copy-start.1 = (s32[1,1,1,32,128]{4,3,2,1,0:T(8,128)S(1)}, s32[1,1,1,32,128]{4,3,2,1,0:T(8,128)}, u32[]{:S(2)}) copy-start(s32[1,1,1,32,128]{4,3,2,1,0:T(8,128)} %param.11) | copy-start | bytes 49156
  13.8 15.5 %collective-permute-start.2 = (f32[3,1,1,32,9,128]{5,3,4,2,1,0:T(8,128)S(1)}, f32[3,1,1,32,9,128]{5,3,4,2,1,0:T(8,128)S(1)}, u32[]{:S(2)}, u32[]{:S(2)}) collective-permute-start(f32[3,1,1,32,9,128]{5,3,4,2,1,0:T(8,128)S(1)} %constant_dynamic-update-slice_fusion), channel_id=1, source_target_pairs={{0,8},{8,16},{16,24},{24,32},{32,40},{40,48},{48,56},{56,0},{1,9},... | collective-permute-start | bytes 1327112 | tf_op jit(solution)/shard_map/ppermute | solution.py:21
  16.3 12.9 %collective-permute-start.3 = (f32[3,1,1,32,9,128]{5,3,4,2,1,0:T(8,128)S(1)}, f32[3,1,1,32,9,128]{5,3,4,2,1,0:T(8,128)S(1)}, u32[]{:S(2)}, u32[]{:S(2)}) collective-permute-start(f32[3,1,1,32,9,128]{5,3,4,2,1,0:T(8,128)S(1)} %constant_dynamic-update-slice_fusion), channel_id=1, source_target_pairs={{8,0},{16,8},{24,16},{32,24},{40,32},{48,40},{56,48},{0,56},{9,1},... | collective-permute-start | bytes 1327112 | tf_op jit(solution)/shard_map/ppermute | solution.py:24
  20.4 14.6 %copy-start.3 = (s32[1,1,1,2,128]{4,3,2,1,0:T(2,128)S(1)}, s32[1,1,1,2,128]{4,3,2,1,0:T(2,128)}, u32[]{:S(2)}) copy-start(s32[1,1,1,2,128]{4,3,2,1,0:T(2,128)} %param.13) | copy-start | bytes 3076
  29.4 18.0 %collective-permute-start.4 = (f32[3,3,1,32,9,128]{5,3,4,2,1,0:T(8,128)S(1)}, f32[3,3,1,32,9,128]{5,3,4,2,1,0:T(8,128)}, u32[]{:S(2)}, u32[]{:S(2)}) collective-permute-start(f32[3,3,1,32,9,128]{5,3,4,2,1,0:T(8,128)S(1)} %pad_maximum_fusion.2), channel_id=1, source_target_pairs={{0,1},{1,2},{2,3},{3,4},{4,5},{5,6},{6,7},{7,0},{8,9},{9,10},{10,1... | collective-permute-start | bytes 3981320 | tf_op jit(solution)/shard_map/ppermute | solution.py:21
  32.6 17.7 %collective-permute-start.5 = (f32[3,3,1,32,9,128]{5,3,4,2,1,0:T(8,128)S(1)}, f32[3,3,1,32,9,128]{5,3,4,2,1,0:T(8,128)}, u32[]{:S(2)}, u32[]{:S(2)}) collective-permute-start(f32[3,3,1,32,9,128]{5,3,4,2,1,0:T(8,128)S(1)} %pad_maximum_fusion.2), channel_id=1, source_target_pairs={{1,0},{2,1},{3,2},{4,3},{5,4},{6,5},{7,6},{0,7},{9,8},{10,9},{11,1... | collective-permute-start | bytes 3981320 | tf_op jit(solution)/shard_map/ppermute | solution.py:24
  33.5 0.7 copy-start
  52.5 6.6 %copy-start.2 = (s32[1,1,1,128]{3,2,1,0:T(1,128)S(1)}, s32[1,1,1,128]{3,2,1,0:T(1,128)}, u32[]{:S(2)}) copy-start(s32[1,1,1,128]{3,2,1,0:T(1,128)} %param.14) | copy-start | bytes 1540
  135.7 148.8 %collective-permute-start.6 = (f32[1,3,3,32,3,128]{5,3,2,1,0,4:T(8,128)}, f32[1,3,3,32,3,128]{5,3,2,1,0,4:T(8,128)S(1)}, u32[]{:S(2)}, u32[]{:S(2)}) collective-permute-start(f32[1,3,3,32,3,128]{5,3,2,1,0,4:T(8,128)} %bitcast.7), channel_id=1, source_target_pairs={{0,64},{64,128},{128,192},{192,0},{1,65},{65,129},{129,193},{193,1... | collective-permute-start | bytes 1327112 | tf_op jit(solution)/shard_map/ppermute | solution.py:21
  160.9 123.7 %collective-permute-start.7 = (f32[1,3,3,32,3,128]{5,3,2,1,0,4:T(8,128)S(1)}, f32[1,3,3,32,3,128]{5,3,2,1,0,4:T(8,128)S(1)}, u32[]{:S(2)}, u32[]{:S(2)}) collective-permute-start(f32[1,3,3,32,3,128]{5,3,2,1,0,4:T(8,128)S(1)} %bitcast.178), channel_id=1, source_target_pairs={{64,0},{128,64},{192,128},{0,192},{65,1},{129,65},{193,129},{1,193... | collective-permute-start | bytes 1327112 | tf_op jit(solution)/shard_map/ppermute | solution.py:24
  284.7 18.1 %collective-permute-start.8 = (f32[5,1,3,32,3,128]{5,3,2,1,0,4:T(8,128)S(1)}, f32[5,1,3,32,3,128]{5,3,2,1,0,4:T(8,128)S(1)}, u32[]{:S(2)}, u32[]{:S(2)}) collective-permute-start(f32[5,1,3,32,3,128]{5,3,2,1,0,4:T(8,128)S(1)} %get-tuple-element.434), channel_id=1, source_target_pairs={{0,8},{8,16},{16,24},{24,32},{32,40},{40,48},{48,56},{56,0},{1,9},... | collective-permute-start | bytes 2211848 | tf_op jit(solution)/shard_map/ppermute | solution.py:21
  286.0 18.4 %collective-permute-start.9 = (f32[5,1,3,32,3,128]{5,3,2,1,0,4:T(8,128)S(1)}, f32[5,1,3,32,3,128]{5,3,2,1,0,4:T(8,128)S(1)}, u32[]{:S(2)}, u32[]{:S(2)}) collective-permute-start(f32[5,1,3,32,3,128]{5,3,2,1,0,4:T(8,128)S(1)} %get-tuple-element.435), channel_id=1, source_target_pairs={{8,0},{16,8},{24,16},{32,24},{40,32},{48,40},{56,48},{0,56},{9,1},... | collective-permute-start | bytes 2211848 | tf_op jit(solution)/shard_map/ppermute | solution.py:24
  304.6 16.0 %collective-permute-start.10 = (f32[5,5,1,32,3,128]{5,3,2,1,0,4:T(8,128)S(1)}, f32[5,5,1,32,3,128]{5,3,2,1,0,4:T(8,128)S(1)}, u32[]{:S(2)}, u32[]{:S(2)}) collective-permute-start(f32[5,5,1,32,3,128]{5,3,2,1,0,4:T(8,128)S(1)} %get-tuple-element.432), channel_id=1, source_target_pairs={{0,1},{1,2},{2,3},{3,4},{4,5},{5,6},{6,7},{7,0},{8,9},{9,10},{10,1... | collective-permute-start | bytes 3686408 | tf_op jit(solution)/shard_map/ppermute | solution.py:21
  306.9 16.2 %collective-permute-start.11 = (f32[5,5,1,32,3,128]{5,3,2,1,0,4:T(8,128)S(1)}, f32[5,5,1,32,3,128]{5,3,2,1,0,4:T(8,128)S(1)}, u32[]{:S(2)}, u32[]{:S(2)}) collective-permute-start(f32[5,5,1,32,3,128]{5,3,2,1,0,4:T(8,128)S(1)} %get-tuple-element.433), channel_id=1, source_target_pairs={{1,0},{2,1},{3,2},{4,3},{5,4},{6,5},{7,6},{0,7},{9,8},{10,9},{11,1... | collective-permute-start | bytes 3686408 | tf_op jit(solution)/shard_map/ppermute | solution.py:24
Sparse Core Ops, SparseCore 0:
  34.3 247.9 all-reduce.1
where the time goes:
time: 386 us
  waiting for transfers between devices  179 us (46%)
  matrix products  62.4 us (16%)
  starting transfers between devices  44.2 us (11%)
  local copies, waits for them, and re-layouts  43.9 us (11%)
  other arithmetic  40.3 us (10%)
  between operations  14.4 us (4%)
    psum x1, waiting for transfers between devices, shards(): all_moments = lax.psum(placed, ('gx', 'gy', 'gz'))  121 us
    ppermute x6, waiting for transfers between devices, extended(): lax.ppermute(lax.slice_in_dim(block, block.shape[dim] - width, None, axis...  51 us
    dot_general x8, matrix products, add_block(): jnp.dot(part_rows, node_hot, precision=lax.Precision.HIGHEST)  47.4 us
    ppermute x6, starting transfers between devices, extended(): lax.ppermute(lax.slice_in_dim(block, block.shape[dim] - width, None, axis...  36.6 us
    gather x6, local copies, waits for them, and re-layouts, tile_group(): other_tiles = jnp.take(ghosts, target, axis=0)  21.5 us
    mul x6, other arithmetic, tile_force(): weighted = strength[None] * separation  12.4 us
    reduce_sum x6, other arithmetic, tile_force(): return (jnp.sum(weighted, axis=2), -jnp.sum(weighted, axis=1))  12 us
    dot_general x6, matrix products, tile_group(): jnp.einsum('gb,gkn->bkn', react_hot, on_peer, precision=lax.Precision.HIG...  10.6 us
  transfers between devices with their start and end apart: 13, of which 9 were waited for; matrix products, arithmetic and copies ran while one was open for 23% of the time, Pallas kernels for 0%

commit v1 on v0

v1 whole, which is shorter than its diff:
```python
import jax
import jax.numpy as jnp
import ml_dtypes
import numpy as np
from jax import lax
from jax.experimental import pallas as pl
from jax.experimental.pallas import tpu as pltpu
from jax.sharding import PartitionSpec as P

CELLS = 16
PAIR_STRENGTH = 0.1
CORE_SQUARED = 0.2
FAR_STRENGTH = 0.008
DRAG_FLOOR = 0.5

BLOCKS = 32
WIDTH = 128
SLOTS = 128
TILES = 36
CELL_DEV = 16
UNROLL = 4
SIDES = (-1, 0, 1)
F32 = jnp.float32
BF16 = jnp.bfloat16
MESH = pl.DeviceIdType.MESH
NT = (((1,), (1,)), ((), ()))
PAIR_SCALE = float(PAIR_STRENGTH * (1.0 / CORE_SQUARED) ** 1.5)
OWN, ON, OFF = 0, 1, 2


def ghost_slot(dx, dy, role):
    return role * 9 + (dx + 1) * 3 + dy + 1


def dot(first, second):
    return jnp.dot(first, second, preferred_element_type=F32)


def dot_nt(first, second):
    return lax.dot_general(first, second, NT, preferred_element_type=F32)


def head(value):
    return value.astype(BF16).astype(F32)


def pair16(low, high):
    return jnp.concatenate([low, high], axis=0).astype(BF16)


def row_ids(shape):
    return lax.broadcasted_iota(jnp.int32, shape, 0)


def block_rows(tile, last, rows):
    zero = jnp.zeros_like(tile)
    line = jnp.where(rows < 3, tile, zero)
    place = jnp.where((rows >= 3) & (rows < 6), tile, zero)
    burgers = jnp.where(rows == 2, last, pltpu.roll(tile, 2, 0))
    burgers = jnp.where(rows < 3, burgers, zero)
    return line, place, burgers


def prepare_block(i, dom, feats, weights_rows):
    rows = row_ids((8, WIDTH))
    tile = dom[i]
    tile = tile - jnp.where((rows >= 3) & (rows < 6), 0.5, 0.0)
    last = dom[32 + (i >> 3), pl.ds(i & 7, 1), :]
    line, place, burgers = block_rows(tile, last, rows)
    norm = jnp.sum(place * place, axis=0, keepdims=True)
    scale = 1.0 / CORE_SQUARED
    low = line - 2.0 * scale * place
    high = burgers + jnp.where(rows == 3, scale, jnp.where(rows == 4, scale * norm + 1.0, 0.0))
    full = jnp.concatenate([low, high], axis=0)
    first = head(full)
    second = head(full - first)
    third = head(full - first - second)
    stack = jnp.concatenate(
        [first, first, second, first, second, third, jnp.zeros((32, WIDTH), F32)], axis=0
    )
    feats[i] = jnp.transpose(stack).astype(BF16)
    place_first = head(place)
    ones = jnp.where(rows == 0, 1.0, 0.0)
    held = pair16(place_first + ones, place - place_first)
    weights_rows[i] = jnp.concatenate([held, held], axis=1)


def pair_group(group, meta, dom, ghosts, shifts, feats, weights_rows, own_out, peer_out, unroll):
    rows = row_ids((8, WIDTH))
    zero = jnp.zeros((8, WIDTH), F32)
    centre = jnp.where((rows >= 3) & (rows < 6), 0.5, 0.0)
    ones = jnp.where(rows == 0, 1.0, 0.0)
    loaded = []
    for u in range(unroll):
        slot = group * unroll + u
        i = meta[0, slot]
        g = meta[1, slot]
        j = meta[2, slot]
        tile = ghosts[g, j] + shifts[g]
        last = ghosts[g, 32 + (j >> 3), pl.ds(j & 7, 1), :]
        line, place, burgers = block_rows(tile, last, rows)
        norm = jnp.sum(place * place, axis=0, keepdims=True)
        extra = jnp.where(rows == 3, norm, jnp.where(rows == 4, 1.0, 0.0))
        line_1 = head(line)
        line_2 = line - line_1
        burgers_1 = head(burgers)
        burgers_2 = burgers - burgers_1
        place_1 = head(place)
        place_r = place - place_1
        place_2 = head(place_r)
        extra_1 = head(extra)
        extra_r = extra - extra_1
        extra_2 = head(extra_r)
        top = jnp.concatenate(
            [pair16(line_1, zero), pair16(zero, burgers_1), pair16(burgers_1, zero), pair16(zero, line_1)], axis=1
        )
        mid = jnp.concatenate(
            [pair16(line_2, zero), pair16(zero, burgers_2), pair16(burgers_2, zero), pair16(zero, line_2)], axis=1
        )
        products = jnp.concatenate([top, mid, top], axis=0)
        dist_1 = pair16(place_1, extra_1)
        dist_2 = pair16(place_2, extra_2)
        dist_3 = pair16(place_r - place_2, extra_r - extra_2)
        dists = jnp.concatenate([dist_1, dist_2, dist_1, dist_3, dist_2, dist_1], axis=0)
        held = pair16(place_1 + ones, place_r)
        held = jnp.concatenate([held, held], axis=1)
        loaded.append((slot, i, place, products, dists, held))
    outs = []
    for slot, i, place, products, dists, held in loaded:
        feat = feats[i]
        outs.append((dot(feat[:, :48], products), dot(feat[:, :96], dists)))
    strengths = []
    for four, dist in outs:
        inv = lax.rsqrt(dist)
        inv_sq = inv * inv
        line_line = four[:, 0:128]
        burgers_burgers = four[:, 128:256]
        line_burgers = four[:, 256:384]
        burgers_line = four[:, 384:512]
        strength = (inv_sq * inv) * (line_line * burgers_burgers + (line_burgers * burgers_line) * inv_sq)
        high = strength.astype(BF16)
        low = (strength - high.astype(F32)).astype(BF16)
        strengths.append((high, low))
    for (slot, i, place, products, dists, held), (high, low) in zip(loaded, strengths):
        peer = dot(weights_rows[i], jnp.concatenate([high, low], axis=0))
        own = dot_nt(held, jnp.concatenate([high, low], axis=1))
        peer = peer[0:8] + peer[8:16]
        own = own[0:8] + own[8:16]
        home = dom[i] - centre
        own_out[slot] = home * own[0:1] - own
        peer_out[slot] = place * peer[0:1] - peer


def slot_table(slot_out, live):
    keep = row_ids((SLOTS, WIDTH)) < live
    parts = [
        jnp.where(keep, PAIR_SCALE * slot_out[:, 3 + c, :], 0.0) for c in range(3)
    ]
    table = jnp.concatenate(parts, axis=1)
    first = table.astype(BF16)
    return jnp.concatenate([first, (table - first.astype(F32)).astype(BF16)], axis=0)


def slot_hot(targets, base, count):
    ids = row_ids((count, SLOTS)) + base
    hot = jnp.where(ids == targets, 1.0, 0.0).astype(BF16)
    return jnp.concatenate([hot, hot], axis=1)


def moment_block(b, dom, cells, total):
    rows = row_ids((8, WIDTH))
    tile = dom[b]
    last = dom[32 + (b >> 3), pl.ds(b & 7, 1), :]
    line, _, burgers = block_rows(tile, last, rows)
    hot = row_ids((CELL_DEV, WIDTH)) == cells[pl.ds(b, 1), :]
    line_1 = head(line)
    line_2 = line - line_1
    burgers_1 = head(burgers)
    burgers_2 = burgers - burgers_1
    zero = jnp.zeros((CELL_DEV, WIDTH), F32)
    spread = [
        jnp.concatenate([jnp.where(hot, part[k : k + 1], zero) for k in range(3)], axis=0).astype(BF16)
        for part in (line_1, line_2)
    ]
    pad = jnp.zeros((8, WIDTH), F32)
    left = jnp.concatenate([pair16(burgers_1, pad), pair16(burgers_1, pad), pair16(burgers_2, pad)], axis=1)
    right = jnp.concatenate([spread[0], spread[1], spread[0]], axis=1)
    return total + dot_nt(left, right)


def node_onehot(b, nodes, node_hot):
    lows = [
        jnp.where(row_ids((128, WIDTH)) == (nodes[e, pl.ds(b, 1), :] & 127), 1.0, 0.0).astype(BF16)
        for e in range(2)
    ]
    node_hot[b] = jnp.concatenate(lows, axis=1)


def node_block(b, nodes, node_hot, values, count, total):
    ends = []
    for e in range(2):
        high = nodes[e, pl.ds(b, 1), :] >> 7
        hit = row_ids((32, WIDTH)) == high
        parts = [jnp.where(hit, values[c, pl.ds(b, 1), :], 0.0) for c in range(2 * count)]
        ends.append(jnp.concatenate(parts, axis=0).astype(BF16))
    return total + dot_nt(jnp.concatenate(ends, axis=1), node_hot[b])


def far_tables():
    index = np.arange(CELL_DEV)
    inner = np.stack([index // 4, index // 2 % 2, index % 2])
    rel = np.arange(256)
    away = np.stack([rel // 64 * 4, rel // 8 % 8 * 2, rel % 8 * 2])
    delta = away[:, None, None, :] + inner[:, :, None, None] - inner[:, None, :, None]
    delta = (delta + 8) % 16 - 8
    dist = np.sqrt(np.maximum((delta.astype(np.float64) ** 2).sum(0), 1.0))
    far = np.where(np.abs(delta).max(0) > 1, FAR_STRENGTH / dist, 0.0).astype(np.float32)
    far = far.reshape(256, 256)
    first = far.astype(ml_dtypes.bfloat16)
    second = (far - first.astype(np.float32)).astype(ml_dtypes.bfloat16)
    table = np.concatenate([first, first, second], axis=1)
    lanes = np.arange(384)
    part = lanes % 128
    fold = np.zeros((16, 384), np.float32)
    for lane in lanes[part < 48]:
        fold[3 * (lane // 128) + part[lane] // 16, lane] = 1.0
    fold = np.concatenate([fold, fold], axis=1).astype(ml_dtypes.bfloat16)
    return table, fold


def kernel(
    meta, pairs, dom, cells, nodes, far_table, fold, out,
    ghosts, shifts, feats, weights_rows, own_out, peer_out, react, from_on, from_off, from_layer,
    node_hot, node_len, values, group_z, group_xy,
    halo_send, halo_recv, react_send, react_recv, gather_send, gather_recv,
):
    size_x, size_y, size_z = 4, 8, 8
    me_x = lax.axis_index("gx")
    me_y = lax.axis_index("gy")
    me_z = lax.axis_index("gz")
    toward = 1 - 2 * lax.rem(me_z, 2)

    def at_x(d):
        return lax.rem(me_x + d + size_x, size_x)

    def at_y(d):
        return lax.rem(me_y + d + size_y, size_y)

    def at_role(role):
        if role == OWN:
            return me_z
        step = toward if role == ON else -toward
        return lax.rem(me_z + step + size_z, size_z)

    def device(dx, dy, role):
        return (at_x(dx), at_y(dy), at_role(role))

    peers = [
        device(dx, dy, role)
        for role in (OWN, ON, OFF)
        for dx in SIDES
        for dy in SIDES
        if (dx, dy, role) != (0, 0, OWN)
    ]
    peers += [(at_x(2), me_y, me_z)]
    peers += [(me_x, at_y(r), me_z) for r in range(2, size_y - 1)]
    peers += [(me_x, me_y, lax.rem(me_z + r, size_z)) for r in range(2, size_z - 1)]

    barrier = pltpu.get_barrier_semaphore()
    for peer in peers:
        pl.semaphore_signal(barrier, inc=1, device_id=peer, device_id_type=MESH)
    pl.semaphore_wait(barrier, len(peers))

    halo = []

    def send_ghost(source, target, slot):
        copy = pltpu.make_async_remote_copy(
            src_ref=source,
            dst_ref=ghosts.at[slot],
            send_sem=halo_send.at[len(halo)],
            recv_sem=halo_recv.at[slot],
            device_id=target,
            device_id_type=MESH,
        )
        copy.start()
        halo.append(copy)

    def await_ghost(slot):
        pltpu.make_async_remote_copy(
            src_ref=dom,
            dst_ref=ghosts.at[slot],
            send_sem=halo_send.at[0],
            recv_sem=halo_recv.at[slot],
            device_id=device(0, 0, ON),
            device_id_type=MESH,
        ).wait_recv()

    for e in (-1, 1):
        send_ghost(dom, device(0, e, OWN), ghost_slot(0, -e, OWN))
    for e in (-1, 1):
        send_ghost(dom, device(e, 0, OWN), ghost_slot(-e, 0, OWN))
    send_ghost(dom, device(0, 0, OFF), ghost_slot(0, 0, OFF))
    send_ghost(dom, device(0, 0, ON), ghost_slot(0, 0, ON))

    ghosts[ghost_slot(0, 0, OWN)] = dom[...]
    rows = row_ids((8, WIDTH))
    for role in (OWN, ON, OFF):
        away_z = 0 if role == OWN else (toward if role == ON else -toward)
        away_z = jnp.asarray(away_z, jnp.int32).astype(F32) - 0.5
        for dx in SIDES:
            for dy in SIDES:
                shifts[ghost_slot(dx, dy, role)] = jnp.where(
                    rows == 3,
                    dx - 0.5,
                    jnp.where(rows == 4, dy - 0.5, jnp.where(rows == 5, away_z, 0.0)),
                )

    def features(b, carry):
        prepare_block(b, dom, feats, weights_rows)
        return carry

    lax.fori_loop(0, 16, features, 0)

    for dx in (-1, 1):
        slot = ghost_slot(dx, 0, OWN)
        await_ghost(slot)
        send_ghost(ghosts.at[slot], device(0, 0, OFF), ghost_slot(dx, 0, OFF))
        send_ghost(ghosts.at[slot], device(0, 0, ON), ghost_slot(dx, 0, ON))
    for dy in (-1, 1):
        slot = ghost_slot(0, dy, OWN)
        await_ghost(slot)
        for e in (-1, 1):
            send_ghost(ghosts.at[slot], device(e, 0, OWN), ghost_slot(-e, dy, OWN))
        send_ghost(ghosts.at[slot], device(0, 0, OFF), ghost_slot(0, dy, OFF))
        send_ghost(ghosts.at[slot], device(0, 0, ON), ghost_slot(0, dy, ON))

    lax.fori_loop(16, BLOCKS, features, 0)

    for dx in (-1, 1):
        slot = ghost_slot(dx, 0, OFF)
        await_ghost(slot)
        for e in (-1, 1):
            send_ghost(ghosts.at[slot], device(0, e, OWN), ghost_slot(dx, -e, OFF))

    moments = lax.fori_loop(
        0, BLOCKS, lambda b, total: moment_block(b, dom, cells, total), jnp.zeros((16, 48), F32), unroll=2
    )
    group_z[0:8, :] = jnp.concatenate([moments[0:8], jnp.zeros((8, 80), F32)], axis=1)

    for dx in (-1, 1):
        for dy in (-1, 1):
            slot = ghost_slot(dx, dy, OWN)
            await_ghost(slot)
            send_ghost(ghosts.at[slot], device(0, 0, ON), ghost_slot(dx, dy, ON))

    def nodes_of(b, carry):
        node_onehot(b, nodes, node_hot)
        return carry

    lax.fori_loop(0, BLOCKS, nodes_of, 0)
    lines = [dom[0:BLOCKS, k, :] for k in range(3)]
    length = 0.5 * jnp.sqrt(lines[0] * lines[0] + lines[1] * lines[1] + lines[2] * lines[2])
    values[0] = head(length)
    values[1] = length - head(length)
    sums = lax.fori_loop(
        0,
        BLOCKS,
        lambda b, total: node_block(b, nodes, node_hot, values, 1, total),
        jnp.zeros((64, WIDTH), F32),
    )
    node_len[...] = jnp.maximum(sums[0:32] + sums[32:64], DRAG_FLOOR)

    for dx in SIDES:
        for dy in SIDES:
            await_ghost(ghost_slot(dx, dy, ON))
    await_ghost(ghost_slot(0, 0, OFF))
    for dy in (-1, 1):
        await_ghost(ghost_slot(0, dy, OFF))
    for dx in (-1, 1):
        for dy in (-1, 1):
            await_ghost(ghost_slot(dx, dy, OFF))

    gathers = []

    def gather(source, target_ref, target, number):
        copy = pltpu.make_async_remote_copy(
            src_ref=source,
            dst_ref=target_ref,
            send_sem=gather_send.at[number],
            recv_sem=gather_recv.at[number],
            device_id=target,
            device_id_type=MESH,
        )
        copy.start()
        gathers.append(copy)

    def pair_part(first, last):
        def body(group, carry):
            pair_group(
                group, meta, dom, ghosts, shifts, feats, weights_rows, own_out, peer_out, UNROLL
            )
            return carry

        lax.fori_loop(first // UNROLL, last // UNROLL, body, 0)

    for r in range(1, size_z):
        gather(
            group_z.at[pl.ds(0, 8)],
            group_z.at[pl.ds(8 * r, 8)],
            (me_x, me_y, lax.rem(me_z - r + size_z, size_z)),
            r - 1,
        )
    pair_part(0, 48)
    for copy in gathers[0:7]:
        copy.wait_recv()
    for a in range(3):
        group_xy[0, 0, 8 * a : 8 * a + 8, :] = group_z[pl.ds(a, 8, stride=8), :]
    for r in range(1, size_y):
        gather(group_xy.at[0, 0], group_xy.at[0, r], (me_x, at_y(-r), me_z), 6 + r)
    pair_part(48, 88)
    for copy in gathers[7:14]:
        copy.wait_recv()
    for r in range(1, size_x):
        gather(group_xy.at[0], group_xy.at[r], (at_x(-r), me_y, me_z), 13 + r)
    pair_part(88, SLOTS)

    live = meta[4, 0]
    table = slot_table(peer_out, live)
    targets = pairs[3:4, :]
    reacts = []

    def send_react(source, target_ref, target, number):
        copy = pltpu.make_async_remote_copy(
            src_ref=source,
            dst_ref=target_ref,
            send_sem=react_send.at[number],
            recv_sem=react_recv.at[number],
            device_id=target,
            device_id_type=MESH,
        )
        copy.start()
        reacts.append(copy)

    react[ON] = dot(slot_hot(targets, 288, 288), table)
    send_react(react.at[ON], from_on, device(0, 0, ON), 0)
    react[OFF] = dot(slot_hot(targets, 576, 288), table)
    for dx in SIDES:
        for dy in SIDES:
            d = ghost_slot(dx, dy, 0)
            send_react(
                react.at[OFF, pl.ds(32 * d, 32)], from_off.at[pl.ds(32 * d, 32)], device(dx, dy, OFF), 1 + d
            )
    react[OWN] = dot(slot_hot(targets, 0, 288), table)
    reacts[0].wait_recv()
    react[OWN] = react[OWN] + from_on[...]
    sent = [(dx, dy) for dx in SIDES for dy in SIDES if (dx, dy) != (0, 0)]
    for number, (dx, dy) in enumerate(sent):
        d = ghost_slot(dx, dy, 0)
        send_react(
            react.at[OWN, pl.ds(32 * d, 32)], from_layer.at[number], device(dx, dy, OWN), 10 + number
        )

    near = dot(slot_hot(pairs[0:1, :], 0, BLOCKS), slot_table(own_out, live))
    near = near + react[OWN, pl.ds(128, 32), :]

    for copy in gathers[14:17]:
        copy.wait_recv()
    sides = []
    for a in range(3):
        held = group_xy[:, :, 8 * a : 8 * a + 8, :].reshape(256, WIDTH)
        first = held.astype(BF16)
        second = (held - first.astype(F32)).astype(BF16)
        sides.append(jnp.concatenate([first, second, first], axis=0))
    blocks = dot(far_table[...], jnp.concatenate(sides, axis=1))
    source = lax.broadcasted_iota(jnp.int32, (256, 384), 0) >> 4
    lane = lax.broadcasted_iota(jnp.int32, (256, 384), 1) & 15
    blocks = jnp.where(source == lane, blocks, 0.0)
    folded = blocks[0:16]
    for k in range(1, 16):
        folded = folded + blocks[16 * k : 16 * k + 16]
    folded = jnp.concatenate([folded, jnp.zeros((112, 384), F32)], axis=0)
    first = folded.astype(BF16)
    second = (folded - first.astype(F32)).astype(BF16)
    field = dot_nt(fold[...], jnp.concatenate([first, second], axis=1))
    cell = cells[...]
    hits = [cell == m for m in range(CELL_DEV)]
    per_seg = []
    for m in range(9):
        held = jnp.zeros((BLOCKS, WIDTH), F32)
        for k in range(CELL_DEV):
            held = jnp.where(hits[k], field[m : m + 1, k : k + 1], held)
        per_seg.append(held)
    burgers = [dom[0:BLOCKS, 6, :], dom[0:BLOCKS, 7, :], dom[BLOCKS:TILES].reshape(BLOCKS, WIDTH)]
    lines = [dom[0:BLOCKS, k, :] for k in range(3)]
    pulled = [sum(per_seg[3 * a + k] * burgers[k] for k in range(3)) for a in range(3)]
    force = [
        pulled[1] * lines[2] - pulled[2] * lines[1],
        pulled[2] * lines[0] - pulled[0] * lines[2],
        pulled[0] * lines[1] - pulled[1] * lines[0],
    ]

    for copy in reacts[1:]:
        copy.wait_recv()
    for number in range(8):
        near = near + from_layer[number]
    for d in range(9):
        near = near + from_off[pl.ds(32 * d, 32), :]
    for c in range(3):
        half = 0.5 * (force[c] + near[:, 128 * c : 128 * c + 128])
        values[c] = head(half)
        values[3 + c] = half - head(half)
    sums = lax.fori_loop(
        0,
        BLOCKS,
        lambda b, total: node_block(b, nodes, node_hot, values, 3, total),
        jnp.zeros((192, WIDTH), F32),
        unroll=2,
    )
    for c in range(3):
        out[c] = (sums[32 * c : 32 * c + 32] + sums[96 + 32 * c : 128 + 32 * c]) / node_len[...]

    for copy in halo + gathers + reacts:
        copy.wait_send()


def shards(seg_state, seg_cells, seg_nodes, pair_blocks, pair_offsets, pair_count):
    own = seg_state[0, 0, 0]
    tiles = jnp.concatenate([own[:, 3:6], own[:, 0:3], own[:, 6:8]], axis=1)
    dom = jnp.concatenate([tiles, own[:, 8].reshape(4, 8, WIDTH)], axis=0)
    cells = seg_cells[0, 0, 0]
    nodes = seg_nodes[0, 0, 0].reshape(2, BLOCKS, WIDTH)
    first, second = pair_blocks[0, 0, 0, 0], pair_blocks[0, 0, 0, 1]
    codes = pair_offsets[0, 0, 0]
    toward = 1 - 2 * (lax.axis_index("gz") % 2)
    away_z = codes % 3 - 1
    role = jnp.where(away_z == 0, OWN, jnp.where(away_z == toward, ON, OFF))
    domain = role * 9 + codes // 3
    live = jnp.broadcast_to(pair_count[0, 0, 0], (SLOTS,))
    empty = jnp.zeros_like(codes)
    meta = jnp.stack([first, domain, second, domain * BLOCKS + second, live, empty, empty, empty])
    far_table, fold = far_tables()
    vmem = pl.BlockSpec(memory_space=pltpu.VMEM)
    out = pl.pallas_call(
        kernel,
        out_shape=jax.ShapeDtypeStruct((3, BLOCKS, WIDTH), F32),
        in_specs=[pl.BlockSpec(memory_space=pltpu.SMEM)] + [vmem] * 6,
        out_specs=vmem,
        scratch_shapes=[
            pltpu.VMEM((27, TILES, 8, WIDTH), F32),
            pltpu.VMEM((27, 8, WIDTH), F32),
            pltpu.VMEM((BLOCKS, 128, WIDTH), BF16),
            pltpu.VMEM((BLOCKS, 16, 256), BF16),
            pltpu.VMEM((SLOTS, 8, WIDTH), F32),
            pltpu.VMEM((SLOTS, 8, WIDTH), F32),
            pltpu.VMEM((3, 288, 384), F32),
            pltpu.VMEM((288, 384), F32),
            pltpu.VMEM((288, 384), F32),
            pltpu.VMEM((8, 32, 384), F32),
            pltpu.VMEM((BLOCKS, 128, 256), BF16),
            pltpu.VMEM((32, WIDTH), F32),
            pltpu.VMEM((6, BLOCKS, WIDTH), F32),
            pltpu.VMEM((64, WIDTH), F32),
            pltpu.VMEM((4, 8, 24, WIDTH), F32),
            pltpu.SemaphoreType.DMA((26,)),
            pltpu.SemaphoreType.DMA((27,)),
            pltpu.SemaphoreType.DMA((18,)),
            pltpu.SemaphoreType.DMA((18,)),
            pltpu.SemaphoreType.DMA((17,)),
            pltpu.SemaphoreType.DMA((17,)),
        ],
        compiler_params=pltpu.CompilerParams(
            collective_id=0, has_side_effects=True, vmem_limit_bytes=40 * 1024 * 1024
        ),
    )(meta, meta, dom, cells, nodes, jnp.asarray(far_table), jnp.asarray(fold))
    return out.reshape(1, 1, 1, 3, BLOCKS * WIDTH)


def solution(mesh):
    placed = (
        P("gx", "gy", "gz", None, None, None),
        P("gx", "gy", "gz", None, None),
        P("gx", "gy", "gz", None, None),
        P("gx", "gy", "gz", None, None),
        P("gx", "gy", "gz", None),
        P("gx", "gy", "gz"),
    )
    return jax.shard_map(
        shards,
        mesh=mesh,
        in_specs=placed,
        out_specs=P("gx", "gy", "gz", None, None),
        check_vma=False,
    )
```

time: 386 us -> 67.7 us (0.18)
  waiting for transfers between devices: 179 us -> 0 us
  Pallas kernels: 0 us -> 62.8 us
  matrix products: 62.4 us -> 0 us
  starting transfers between devices: 44.2 us -> 0 us
  other arithmetic: 40.3 us -> 0.07 us
  local copies, waits for them, and re-layouts: 43.9 us -> 3.9 us
  between operations: 14.4 us -> 0.74 us
    psum x1 -> x0, waiting for transfers between devices: 121 us -> none  [shards(): all_moments = lax.psum(placed, ('gx', 'gy', 'gz'))]
    pallas_call x0 -> x1, Pallas kernels: none -> 62.8 us  [shards(): pl.pallas_call(kernel, out_shape=jax.ShapeDtypeStruct((3, BLOCKS, WIDTH),...]
    dot_general x23 -> x0, matrix products: 62.4 us -> none  [the longest x8 47.4 us: add_block(): jnp.dot(part_rows, node_hot, precision=lax.Precision.HIGHEST)]
    ppermute x12 -> x0, waiting for transfers between devices: 57.9 us -> none  [the longest x6 51 us: extended(): lax.ppermute(lax.slice_in_dim(block, block.shape[dim] - width, None, axis...]
    ppermute x12 -> x0, starting transfers between devices: 44.2 us -> none  [the longest x6 36.6 us: extended(): lax.ppermute(lax.slice_in_dim(block, block.shape[dim] - width, None, axis...]
    gather x12 -> x0, local copies, waits for them, and re-layouts: 24.9 us -> none  [the longest x6 21.5 us: tile_group(): other_tiles = jnp.take(ghosts, target, axis=0)]
    mul x8 -> x0, other arithmetic: 12.5 us -> none  [the longest x6 12.4 us: tile_force(): weighted = strength[None] * separation]
    reduce_sum x7 -> x0, other arithmetic: 12.1 us -> none  [the longest x6 12 us: tile_force(): return (jnp.sum(weighted, axis=2), -jnp.sum(weighted, axis=1))]
  transfers between devices with their start and end apart: 13 -> 0, of which waited for: 9 -> 0; matrix products, arithmetic and copies ran while one was open for 23% -> 0% of each run, Pallas kernels for 0% -> 0%
where the time goes in v1:
time: 67.7 us; the launch traced here: 67.5 us
  Pallas kernels  62.8 us (93%)
  local copies, waits for them, and re-layouts  3.9 us (6%)
  between operations  0.74 us (1%)
    pallas_call x1, Pallas kernels, shards(): pl.pallas_call(kernel, out_shape=jax.ShapeDtypeStruct((3, BLOCKS, WIDTH),...  62.8 us
    unnamed x15, local copies, waits for them, and re-layouts  3.81 us

profile of v1, /device:TPU:1, one launch (start us, length us, event | category | flops | bytes accessed | tf_op | source)
XLA Modules:
  0.0 67.5 jit_solution(9162433433966291364)
XLA Ops:
  0.0 0.0 copy-start.4
  0.0 0.0 copy-start.5
  0.0 0.7 copy-done.4
  0.7 0.0 copy-done.5
  1.4 1.0 %copy.16 = f32[1,1,1,32,9,128]{5,4,3,2,1,0:T(8,128)S(1)} copy(f32[1,1,1,32,9,128]{5,3,4,2,1,0:T(8,128)} %param.8) | data formatting | bytes 294912 | tf_op args[0]
  2.4 0.0 copy-start
  2.5 0.0 copy-start.3
  2.6 0.7 %copy-done.3 = s32[1,1,1,2,4096]{4,3,2,1,0:T(2,128)S(1)} copy-done((s32[1,1,1,2,4096]{4,3,2,1,0:T(2,128)S(1)}, s32[1,1,1,2,4096]{4,3,2,1,0:T(2,128)}, u32[]{:S(2)}) %copy-start.3) | copy-done | bytes 32792
  3.3 0.0 copy-start.1
  3.3 0.0 copy-start.2
  3.3 0.1 copy-done
  3.4 0.6 copy-done.1
  4.1 0.0 copy-done.2
  4.1 62.8 %shard_map.82 = f32[3,32,128]{2,1,0:T(8,128)S(1)} custom-call(s32[8,128]{1,0:T(8,128)S(1)} %stack.9.meta.pairs, s32[8,128]{1,0:T(8,128)S(1)} %stack.9.meta.pairs, f32[36,8,128]{2,1,0:T(8,128)S(1)} %pad_maximum_fusion.dom, s32[32,128]{1,0:T(8,128)S(1)} %bitcast.36, s32[2,32,128]{2,1,0:T(8,128)S(1)} %bitcast.35, bf16[256,768]{1,0:T(8,128)(2,1)S(1)} %copy-done, ...), custom_call_target="tpu_custom_call" | custom-call | tf_op jit(solution)/shard_map/pallas_call | solution.py:543
  66.9 0.6 copy.20
  (11 shorter events, 0.2 us)
Async XLA Ops:
  0.0 0.7 %copy-start.4 = (s32[1,1,1,2,128]{4,3,2,1,0:T(2,128)S(1)}, s32[1,1,1,2,128]{4,3,2,1,0:T(2,128)}, u32[]{:S(2)}) copy-start(s32[1,1,1,2,128]{4,3,2,1,0:T(2,128)} %param.11) | copy-start | bytes 3076
  0.0 0.7 %copy-start.5 = (s32[1,1,1,128]{3,2,1,0:T(1,128)S(1)}, s32[1,1,1,128]{3,2,1,0:T(1,128)}, u32[]{:S(2)}) copy-start(s32[1,1,1,128]{3,2,1,0:T(1,128)} %param.12) | copy-start | bytes 1540
  2.4 1.0 %copy-start = (bf16[256,768]{1,0:T(8,128)(2,1)S(1)}, bf16[256,768]{1,0:T(8,128)(2,1)}, u32[]{:S(2)}) copy-start(bf16[256,768]{1,0:T(8,128)(2,1)} %constant.50.clone.far_table) | copy-start | bytes 1179652
  2.5 0.8 %copy-start.3 = (s32[1,1,1,2,4096]{4,3,2,1,0:T(2,128)S(1)}, s32[1,1,1,2,4096]{4,3,2,1,0:T(2,128)}, u32[]{:S(2)}) copy-start(s32[1,1,1,2,4096]{4,3,2,1,0:T(2,128)} %param.10) | copy-start | bytes 98308
  3.3 0.8 %copy-start.1 = (bf16[16,768]{1,0:T(8,128)(2,1)S(1)}, bf16[16,768]{1,0:T(8,128)(2,1)}, u32[]{:S(2)}) copy-start(bf16[16,768]{1,0:T(8,128)(2,1)} %constant.51.clone.fold) | copy-start | bytes 73732
  3.3 0.8 %copy-start.2 = (s32[1,1,1,32,128]{4,3,2,1,0:T(8,128)S(1)}, s32[1,1,1,32,128]{4,3,2,1,0:T(8,128)}, u32[]{:S(2)}) copy-start(s32[1,1,1,32,128]{4,3,2,1,0:T(8,128)} %param.9) | copy-start | bytes 49156

commit v2 on v1

v2 whole, which is shorter than its diff:
```python
import jax
import jax.numpy as jnp
import ml_dtypes
import numpy as np
from jax import lax
from jax.experimental import pallas as pl
from jax.experimental.pallas import tpu as pltpu
from jax.sharding import PartitionSpec as P

CELLS = 16
PAIR_STRENGTH = 0.1
CORE_SQUARED = 0.2
FAR_STRENGTH = 0.008
DRAG_FLOOR = 0.5

BLOCKS = 32
WIDTH = 128
SLOTS = 128
TILES = 36
CELL_DEV = 16
UNROLL = 8
SIDES = (-1, 0, 1)
F32 = jnp.float32
BF16 = jnp.bfloat16
MESH = pl.DeviceIdType.MESH
NT = (((1,), (1,)), ((), ()))
PAIR_SCALE = float(PAIR_STRENGTH * (1.0 / CORE_SQUARED) ** 1.5)
OWN, ON, OFF = 0, 1, 2


def ghost_slot(dx, dy, role):
    return role * 9 + (dx + 1) * 3 + dy + 1


def dot(first, second):
    return jnp.dot(first, second, preferred_element_type=F32)


def dot_nt(first, second):
    return lax.dot_general(first, second, NT, preferred_element_type=F32)


def head(value):
    return value.astype(BF16).astype(F32)


def pair16(low, high):
    return jnp.concatenate([low, high], axis=0).astype(BF16)


def row_ids(shape):
    return lax.broadcasted_iota(jnp.int32, shape, 0)


def block_rows(tile, last, rows):
    zero = jnp.zeros_like(tile)
    middle = (rows >= 3) & (rows < 6)
    line = jnp.where(middle, tile, zero)
    place = jnp.where(rows < 3, tile, zero)
    burgers = jnp.where(rows == 5, last, pltpu.roll(tile, 5, 0))
    burgers = jnp.where(middle, burgers, zero)
    return line, place, burgers


def prepare_block(i, dom, feats, weights_rows):
    rows = row_ids((8, WIDTH))
    tile = dom[i]
    tile = tile - jnp.where(rows < 3, 0.5, 0.0)
    last = dom[32 + (i >> 3), pl.ds(i & 7, 1), :]
    line, place, burgers = block_rows(tile, last, rows)
    norm = jnp.sum(place * place, axis=0, keepdims=True)
    scale = 1.0 / CORE_SQUARED
    low = line - 2.0 * scale * place
    high = burgers + jnp.where(rows == 0, scale, jnp.where(rows == 1, scale * norm + 1.0, 0.0))
    full = jnp.concatenate([low, high], axis=0)
    first = head(full)
    second = head(full - first)
    third = head(full - first - second)
    stack = jnp.concatenate(
        [first, first, second, first, second, third, jnp.zeros((32, WIDTH), F32)], axis=0
    )
    feats[i] = jnp.transpose(stack).astype(BF16)
    place_first = head(place)
    ones = jnp.where(rows == 3, 1.0, 0.0)
    held = pair16(place_first + ones, place - place_first)
    weights_rows[i] = jnp.concatenate([held, held], axis=1)


def pair_group(group, blocks, codes, dom, ghosts, shifts, feats, weights_rows, own_out, peer_out, unroll):
    rows = row_ids((8, WIDTH))
    zero = jnp.zeros((8, WIDTH), F32)
    centre = jnp.where(rows < 3, 0.5, 0.0)
    ones = jnp.where(rows == 3, 1.0, 0.0)
    loaded = []
    for u in range(unroll):
        slot = group * unroll + u
        i = blocks[0, slot]
        g = codes[0, slot]
        j = blocks[1, slot]
        tile = ghosts[g, j] + shifts[g]
        last = ghosts[g, 32 + (j >> 3), pl.ds(j & 7, 1), :]
        line, place, burgers = block_rows(tile, last, rows)
        norm = jnp.sum(place * place, axis=0, keepdims=True)
        extra = jnp.where(rows == 0, norm, jnp.where(rows == 1, 1.0, 0.0))
        line_1 = head(line)
        line_2 = line - line_1
        burgers_1 = head(burgers)
        burgers_2 = burgers - burgers_1
        place_1 = head(place)
        place_r = place - place_1
        place_2 = head(place_r)
        extra_1 = head(extra)
        extra_r = extra - extra_1
        extra_2 = head(extra_r)
        top = jnp.concatenate(
            [pair16(line_1, zero), pair16(zero, burgers_1), pair16(burgers_1, zero), pair16(zero, line_1)], axis=1
        )
        mid = jnp.concatenate(
            [pair16(line_2, zero), pair16(zero, burgers_2), pair16(burgers_2, zero), pair16(zero, line_2)], axis=1
        )
        products = jnp.concatenate([top, mid, top], axis=0)
        dist_1 = pair16(place_1, extra_1)
        dist_2 = pair16(place_2, extra_2)
        dist_3 = pair16(place_r - place_2, extra_r - extra_2)
        dists = jnp.concatenate([dist_1, dist_2, dist_1, dist_3, dist_2, dist_1], axis=0)
        held = pair16(place_1 + ones, place_r)
        held = jnp.concatenate([held, held], axis=1)
        loaded.append((slot, i, place, products, dists, held))
    outs = []
    for slot, i, place, products, dists, held in loaded:
        feat = feats[i]
        outs.append((dot(feat[:, :48], products), dot(feat[:, :96], dists)))
    strengths = []
    for four, dist in outs:
        inv = lax.rsqrt(dist)
        inv_sq = inv * inv
        line_line = four[:, 0:128]
        burgers_burgers = four[:, 128:256]
        line_burgers = four[:, 256:384]
        burgers_line = four[:, 384:512]
        strength = (inv_sq * inv) * (line_line * burgers_burgers + (line_burgers * burgers_line) * inv_sq)
        high = strength.astype(BF16)
        low = (strength - high.astype(F32)).astype(BF16)
        strengths.append((high, low))
    for (slot, i, place, products, dists, held), (high, low) in zip(loaded, strengths):
        peer = dot(weights_rows[i], jnp.concatenate([high, low], axis=0))
        own = dot_nt(held, jnp.concatenate([high, low], axis=1))
        peer = peer[0:8] + peer[8:16]
        own = own[0:8] + own[8:16]
        home = dom[i] - centre
        own_out[slot] = home * own[3:4] - own
        peer_out[slot] = place * peer[3:4] - peer


def slot_table(slot_out, live):
    keep = row_ids((SLOTS, WIDTH)) < live
    parts = [
        jnp.where(keep, PAIR_SCALE * slot_out[:, c, :], 0.0) for c in range(3)
    ]
    table = jnp.concatenate(parts, axis=1)
    first = table.astype(BF16)
    return jnp.concatenate([first, (table - first.astype(F32)).astype(BF16)], axis=0)


def slot_hot(targets, base, count):
    ids = row_ids((count, SLOTS)) + base
    hot = jnp.where(ids == targets, 1.0, 0.0).astype(BF16)
    return jnp.concatenate([hot, hot], axis=1)


def moment_block(b, dom, cells, total):
    rows = row_ids((8, WIDTH))
    tile = dom[b]
    last = dom[32 + (b >> 3), pl.ds(b & 7, 1), :]
    line, _, burgers = block_rows(tile, last, rows)
    hot = row_ids((CELL_DEV, WIDTH)) == cells[pl.ds(b, 1), :]
    line_1 = head(line)
    line_2 = line - line_1
    burgers_1 = head(burgers)
    burgers_2 = burgers - burgers_1
    zero = jnp.zeros((CELL_DEV, WIDTH), F32)
    spread = [
        jnp.concatenate([jnp.where(hot, part[3 + k : 4 + k], zero) for k in range(3)], axis=0).astype(BF16)
        for part in (line_1, line_2)
    ]
    pad = jnp.zeros((8, WIDTH), F32)
    left = jnp.concatenate([pair16(burgers_1, pad), pair16(burgers_1, pad), pair16(burgers_2, pad)], axis=1)
    right = jnp.concatenate([spread[0], spread[1], spread[0]], axis=1)
    return total + dot_nt(left, right)


def nodes_row(nodes, e, b):
    return nodes[e : e + 1, pl.ds(pl.multiple_of(b * WIDTH, WIDTH), WIDTH)]


def node_onehot(b, nodes, node_hot):
    lows = [
        jnp.where(row_ids((128, WIDTH)) == (nodes_row(nodes, e, b) & 127), 1.0, 0.0).astype(BF16)
        for e in range(2)
    ]
    node_hot[b] = jnp.concatenate(lows, axis=1)


def node_sums(nodes, node_hot, values, count):
    together = 4

    def body(turn, total):
        parts, hots = [], []
        for u in range(together):
            b = turn * together + u
            for e in range(2):
                hit = row_ids((32, WIDTH)) == nodes_row(nodes, e, b) >> 7
                rows = [jnp.where(hit, values[c, pl.ds(b, 1), :], 0.0) for c in range(2 * count)]
                parts.append(jnp.concatenate(rows, axis=0).astype(BF16))
            hots.append(node_hot[b])
        return total + dot_nt(jnp.concatenate(parts, axis=1), jnp.concatenate(hots, axis=1))

    return lax.fori_loop(0, BLOCKS // together, body, jnp.zeros((64 * count, WIDTH), F32))


def far_tables():
    index = np.arange(CELL_DEV)
    inner = np.stack([index // 4, index // 2 % 2, index % 2])
    rel = np.arange(256)
    away = np.stack([rel // 64 * 4, (rel // 8 % 8 - 3) * 2, (rel % 8 - 3) * 2])
    delta = away[:, None, None, :] + inner[:, :, None, None] - inner[:, None, :, None]
    delta = (delta + 8) % 16 - 8
    dist = np.sqrt(np.maximum((delta.astype(np.float64) ** 2).sum(0), 1.0))
    far = np.where(np.abs(delta).max(0) > 1, FAR_STRENGTH / dist, 0.0).astype(np.float32)
    far = far.reshape(256, 256)
    first = far.astype(ml_dtypes.bfloat16)
    second = (far - first.astype(np.float32)).astype(ml_dtypes.bfloat16)
    table = np.concatenate([first, first, second], axis=1)
    lanes = np.arange(384)
    part = lanes % 128
    fold = np.zeros((16, 384), np.float32)
    for lane in lanes[part < 48]:
        fold[3 * (lane // 128) + part[lane] // 16, lane] = 1.0
    fold = np.concatenate([fold, fold], axis=1).astype(ml_dtypes.bfloat16)
    return table, fold


def kernel(
    state_in, cells_in, nodes_in, blocks_in, codes_in, count, far_in, fold_in, out,
    raw, cells, nodes, block_ids, code_ids, blocks, codes, far_table, fold,
    dom, ghosts, shifts, feats, weights_rows, own_out, peer_out, react, from_on, from_off, from_layer,
    node_hot, node_len, values, group_z, group_xy,
    load_sem, halo_send, halo_recv, react_send, react_recv, gather_send, gather_recv,
):
    size_x, size_y, size_z = 4, 8, 8
    me_x = lax.axis_index("gx")
    me_y = lax.axis_index("gy")
    me_z = lax.axis_index("gz")
    toward = 1 - 2 * lax.rem(me_z, 2)

    loads = [
        pltpu.make_async_copy(source, target, load_sem.at[number])
        for number, (source, target) in enumerate(
            [
                (state_in, raw), (cells_in, cells), (nodes_in, nodes), (blocks_in, blocks), (codes_in, codes),
                (blocks_in, block_ids), (codes_in, code_ids), (far_in, far_table), (fold_in, fold),
            ]
        )
    ]
    for load in loads:
        load.start()

    def at_x(d):
        return lax.rem(me_x + d + size_x, size_x)

    def at_y(d):
        return lax.rem(me_y + d + size_y, size_y)

    def at_z(d):
        return lax.rem(me_z + d + size_z, size_z)

    def away(role):
        return 0 if role == OWN else (toward if role == ON else -toward)

    def device(dx, dy, role):
        return (at_x(dx), at_y(dy), at_z(away(role)))

    def code(dx, dy, dz):
        return (dx + 1) * 9 + (dy + 1) * 3 + dz + 1

    peers = [
        device(-1, 0, OWN), device(1, 0, OWN), device(0, -1, OWN), device(0, 1, OWN), device(0, 0, OFF), device(0, 0, ON)
    ]
    barrier = pltpu.get_barrier_semaphore()
    for peer in peers:
        pl.semaphore_signal(barrier, inc=1, device_id=peer, device_id_type=MESH)
    loads[0].wait()
    for k in range(8):
        dom[0:BLOCKS, k, :] = raw[k]
    dom[BLOCKS:TILES] = raw[8].reshape(4, 8, WIDTH)
    pl.semaphore_wait(barrier, len(peers))

    halo = []
    half = TILES // 2

    def piece(ref, part):
        return ref if part is None else ref.at[pl.ds(part * half, half)]

    def ghost(dx, dy, role):
        return ghosts.at[code(dx, dy, away(role))]

    def send_ghost(source, to, slot, offset, part):
        copy = pltpu.make_async_remote_copy(
            src_ref=piece(source, part),
            dst_ref=piece(ghosts.at[code(*offset)], part),
            send_sem=halo_send.at[len(halo)],
            recv_sem=halo_recv.at[2 * slot + (part or 0)],
            device_id=device(*to),
            device_id_type=MESH,
        )
        copy.start()
        halo.append(copy)

    def await_ghost(dx, dy, role, part=None):
        pltpu.make_async_remote_copy(
            src_ref=piece(dom, part),
            dst_ref=piece(ghost(dx, dy, role), part),
            send_sem=halo_send.at[0],
            recv_sem=halo_recv.at[2 * ghost_slot(dx, dy, role) + (part or 0)],
            device_id=device(0, 0, ON),
            device_id_type=MESH,
        ).wait_recv()

    def pass_x(source, e, dy, role, part):
        send_ghost(source, (e, 0, OWN), ghost_slot(-e, dy, role), (-e, dy, away(role)), part)

    def pass_y(source, e, dx, role, part):
        send_ghost(source, (0, e, OWN), ghost_slot(dx, -e, role), (dx, -e, away(role)), part)

    def pass_off(source, dx, dy, part):
        send_ghost(source, (0, 0, OFF), ghost_slot(dx, dy, OFF), (dx, dy, toward), part)

    def pass_on(source, dx, dy):
        send_ghost(source, (0, 0, ON), ghost_slot(dx, dy, ON), (dx, dy, -toward), None)

    for part in (0, 1):
        for e in (-1, 1):
            pass_y(dom, e, 0, OWN, part)
        for e in (-1, 1):
            pass_x(dom, e, 0, OWN, part)
        pass_off(dom, 0, 0, part)
    pass_on(dom, 0, 0)

    gathers = []

    def gather(source, target, to):
        number = len(gathers)
        copy = pltpu.make_async_remote_copy(
            src_ref=source,
            dst_ref=target,
            send_sem=gather_send.at[number],
            recv_sem=gather_recv.at[number],
            device_id=to,
            device_id_type=MESH,
        )
        copy.start()
        gathers.append(copy)
        return copy

    def spread_of_8(ref_of, at):
        for distance, moves in (
            (1, ((3, 4, 1, -1), (3, 2, 1, 1))),
            (2, ((3, 5, 2, -1), (2, 0, 2, 1))),
            (2, ((5, 7, 1, -1),)),
        ):
            sent = [
                gather(ref_of(first, count), ref_of(target, count), at(sign * distance))
                for first, target, count, sign in moves
            ]
            yield
            for copy in sent:
                copy.wait_recv()

    def gather_steps():
        yield from spread_of_8(
            lambda first, count: group_z.at[pl.ds(8 * first, 8 * count)], lambda d: (me_x, me_y, at_z(d))
        )
        for a in range(3):
            group_xy[0, 3, 8 * a : 8 * a + 8, :] = group_z[pl.ds(3 + a, 8, stride=8), :]
        yield from spread_of_8(
            lambda first, count: group_xy.at[0, pl.ds(first, count)], lambda d: (me_x, at_y(d), me_z)
        )
        sent = [
            gather(group_xy.at[0], group_xy.at[r], (at_x(-r), me_y, me_z)) for r in range(1, size_x)
        ]
        yield
        for copy in sent:
            copy.wait_recv()

    steps = gather_steps()

    def gather_step():
        next(steps, None)

    def features(b, carry):
        prepare_block(b, dom, feats, weights_rows)
        return carry

    def features_part(number):
        lax.fori_loop(4 * number, 4 * number + 4, features, 0, unroll=2)

    def nodes_of(b, carry):
        node_onehot(b, nodes, node_hot)
        return carry

    loads[1].wait()
    moments = lax.fori_loop(
        0, BLOCKS, lambda b, total: moment_block(b, dom, cells, total), jnp.zeros((16, 48), F32), unroll=4
    )
    group_z[24:32, :] = jnp.concatenate([moments[0:8], jnp.zeros((8, 80), F32)], axis=1)
    gather_step()

    for part in (0, 1):
        await_ghost(0, 0, OFF, part)
        for e in (-1, 1):
            pass_x(ghost(0, 0, OFF), e, 0, OFF, part)
    features_part(0)
    for part in (0, 1):
        for dx in (-1, 1):
            await_ghost(dx, 0, OWN, part)
            pass_y(ghost(dx, 0, OWN), -dx, dx, OWN, part)
    for dx in (-1, 1):
        pass_on(ghost(dx, 0, OWN), dx, 0)
    gather_step()
    features_part(1)
    for part in (0, 1):
        for dy in (-1, 1):
            await_ghost(0, dy, OWN, part)
            pass_x(ghost(0, dy, OWN), dy, dy, OWN, part)
            pass_off(ghost(0, dy, OWN), 0, dy, part)
    for dy in (-1, 1):
        pass_on(ghost(0, dy, OWN), 0, dy)
    gather_step()
    features_part(2)
    for part in (0, 1):
        for dx in (-1, 1):
            await_ghost(dx, 0, OFF, part)
            pass_y(ghost(dx, 0, OFF), dx, dx, OFF, part)
    features_part(3)
    gather_step()
    for part in (0, 1):
        for d in (-1, 1):
            await_ghost(d, d, OWN, part)
            pass_off(ghost(d, d, OWN), d, d, part)
    for d in (-1, 1):
        pass_on(ghost(d, d, OWN), d, d)
    features_part(4)
    for d in (-1, 1):
        for part in (0, 1):
            await_ghost(d, -d, OWN, part)
        pass_on(ghost(d, -d, OWN), d, -d)
    gather_step()
    for number in range(5, 8):
        features_part(number)

    ghosts[code(0, 0, 0)] = dom[...]
    rows = row_ids((8, WIDTH))
    for dx in SIDES:
        for dy in SIDES:
            for dz in SIDES:
                shifts[code(dx, dy, dz)] = jnp.where(
                    rows == 0,
                    dx - 0.5,
                    jnp.where(rows == 1, dy - 0.5, jnp.where(rows == 2, dz - 0.5, 0.0)),
                )
    loads[2].wait()
    lax.fori_loop(0, BLOCKS, nodes_of, 0, unroll=2)
    gather_step()
    lines = [raw[3 + k] for k in range(3)]
    length = 0.5 * jnp.sqrt(lines[0] * lines[0] + lines[1] * lines[1] + lines[2] * lines[2])
    values[0] = head(length)
    values[1] = length - head(length)
    sums = node_sums(nodes, node_hot, values, 1)
    node_len[...] = jnp.maximum(sums[0:32] + sums[32:64], DRAG_FLOOR)
    for load in loads[3:]:
        load.wait()

    for part in (0, 1):
        for dy in (-1, 1):
            await_ghost(0, dy, OFF, part)
        for d in (-1, 1):
            await_ghost(d, -d, OFF, part)
            await_ghost(d, d, OFF, part)
    for dx in SIDES:
        for dy in SIDES:
            await_ghost(dx, dy, ON)

    def pair_part(first, last):
        def body(group, carry):
            pair_group(
                group, blocks, codes, dom, ghosts, shifts, feats, weights_rows, own_out, peer_out, UNROLL
            )
            return carry

        lax.fori_loop(first // UNROLL, last // UNROLL, body, 0)

    pair_part(0, 64)
    gather_step()
    pair_part(64, SLOTS)

    live = count[0]
    table = slot_table(peer_out, live)
    code_row = code_ids[...]
    side = (code_row * 43) >> 7
    away_z = code_row - 3 * side - 1
    role_row = jnp.where(away_z == 0, OWN, jnp.where(away_z == toward, ON, OFF))
    targets = (role_row * 9 + side) * BLOCKS + block_ids[1:2, :]
    reacts = []

    def send_react(source, target_ref, target, number):
        copy = pltpu.make_async_remote_copy(
            src_ref=source,
            dst_ref=target_ref,
            send_sem=react_send.at[number],
            recv_sem=react_recv.at[number],
            device_id=target,
            device_id_type=MESH,
        )
        copy.start()
        reacts.append(copy)

    react[ON] = dot(slot_hot(targets, 288, 288), table)
    send_react(react.at[ON], from_on, device(0, 0, ON), 0)
    react[OFF] = dot(slot_hot(targets, 576, 288), table)
    for dx in SIDES:
        for dy in SIDES:
            d = ghost_slot(dx, dy, 0)
            send_react(
                react.at[OFF, pl.ds(32 * d, 32)], from_off.at[pl.ds(32 * d, 32)], device(dx, dy, OFF), 1 + d
            )
    react[OWN] = dot(slot_hot(targets, 0, 288), table)
    reacts[0].wait_recv()
    react[OWN] = react[OWN] + from_on[...]
    sent = [(dx, dy) for dx in SIDES for dy in SIDES if (dx, dy) != (0, 0)]
    for number, (dx, dy) in enumerate(sent):
        d = ghost_slot(dx, dy, 0)
        send_react(
            react.at[OWN, pl.ds(32 * d, 32)], from_layer.at[number], device(dx, dy, OWN), 10 + number
        )

    near = dot(slot_hot(block_ids[0:1, :], 0, BLOCKS), slot_table(own_out, live))
    near = near + react[OWN, pl.ds(128, 32), :]

    for _ in steps:
        pass
    sides = []
    for a in range(3):
        held = group_xy[:, :, 8 * a : 8 * a + 8, :].reshape(256, WIDTH)
        first = held.astype(BF16)
        second = (held - first.astype(F32)).astype(BF16)
        sides.append(jnp.concatenate([first, second, first], axis=0))
    spread = dot(far_table[...], jnp.concatenate(sides, axis=1))
    source = lax.broadcasted_iota(jnp.int32, (256, 384), 0) >> 4
    lane = lax.broadcasted_iota(jnp.int32, (256, 384), 1) & 15
    spread = jnp.where(source == lane, spread, 0.0)
    folded = spread[0:16]
    for k in range(1, 16):
        folded = folded + spread[16 * k : 16 * k + 16]
    folded = jnp.concatenate([folded, jnp.zeros((112, 384), F32)], axis=0)
    first = folded.astype(BF16)
    second = (folded - first.astype(F32)).astype(BF16)
    field = dot_nt(fold[...], jnp.concatenate([first, second], axis=1))
    cell = cells[...]
    hits = [cell == m for m in range(CELL_DEV)]
    per_seg = []
    for m in range(9):
        held = jnp.zeros((BLOCKS, WIDTH), F32)
        for k in range(CELL_DEV):
            held = jnp.where(hits[k], field[m : m + 1, k : k + 1], held)
        per_seg.append(held)
    burgers = [raw[6], raw[7], raw[8]]
    lines = [raw[3 + k] for k in range(3)]
    pulled = [sum(per_seg[3 * a + k] * burgers[k] for k in range(3)) for a in range(3)]
    force = [
        pulled[1] * lines[2] - pulled[2] * lines[1],
        pulled[2] * lines[0] - pulled[0] * lines[2],
        pulled[0] * lines[1] - pulled[1] * lines[0],
    ]

    for copy in reacts[1:]:
        copy.wait_recv()
    for number in range(8):
        near = near + from_layer[number]
    for d in range(9):
        near = near + from_off[pl.ds(32 * d, 32), :]
    for c in range(3):
        half = 0.5 * (force[c] + near[:, 128 * c : 128 * c + 128])
        values[c] = head(half)
        values[3 + c] = half - head(half)
    sums = node_sums(nodes, node_hot, values, 3)
    for c in range(3):
        out[c] = (sums[32 * c : 32 * c + 32] + sums[96 + 32 * c : 128 + 32 * c]) / node_len[...]

    for copy in halo + gathers + reacts:
        copy.wait_send()


def shards(seg_state, seg_cells, seg_nodes, pair_blocks, pair_offsets, pair_count):
    far_table, fold = far_tables()
    anywhere = pl.BlockSpec(memory_space=pltpu.HBM)
    out = pl.pallas_call(
        kernel,
        out_shape=jax.ShapeDtypeStruct((3, BLOCKS, WIDTH), F32),
        in_specs=[anywhere] * 5 + [pl.BlockSpec(memory_space=pltpu.SMEM)] + [anywhere] * 2,
        out_specs=pl.BlockSpec(memory_space=pltpu.VMEM),
        scratch_shapes=[
            pltpu.VMEM((9, BLOCKS, WIDTH), F32),
            pltpu.VMEM((BLOCKS, WIDTH), jnp.int32),
            pltpu.VMEM((2, BLOCKS * WIDTH), jnp.int32),
            pltpu.VMEM((2, SLOTS), jnp.int32),
            pltpu.VMEM((1, SLOTS), jnp.int32),
            pltpu.SMEM((2, SLOTS), jnp.int32),
            pltpu.SMEM((1, SLOTS), jnp.int32),
            pltpu.VMEM(far_table.shape, BF16),
            pltpu.VMEM(fold.shape, BF16),
            pltpu.VMEM((TILES, 8, WIDTH), F32),
            pltpu.VMEM((27, TILES, 8, WIDTH), F32),
            pltpu.VMEM((27, 8, WIDTH), F32),
            pltpu.VMEM((BLOCKS, 128, WIDTH), BF16),
            pltpu.VMEM((BLOCKS, 16, 256), BF16),
            pltpu.VMEM((SLOTS, 8, WIDTH), F32),
            pltpu.VMEM((SLOTS, 8, WIDTH), F32),
            pltpu.VMEM((3, 288, 384), F32),
            pltpu.VMEM((288, 384), F32),
            pltpu.VMEM((288, 384), F32),
            pltpu.VMEM((8, 32, 384), F32),
            pltpu.VMEM((BLOCKS, 128, 256), BF16),
            pltpu.VMEM((32, WIDTH), F32),
            pltpu.VMEM((6, BLOCKS, WIDTH), F32),
            pltpu.VMEM((64, WIDTH), F32),
            pltpu.VMEM((4, 8, 24, WIDTH), F32),
            pltpu.SemaphoreType.DMA((9,)),
            pltpu.SemaphoreType.DMA((43,)),
            pltpu.SemaphoreType.DMA((54,)),
            pltpu.SemaphoreType.DMA((18,)),
            pltpu.SemaphoreType.DMA((18,)),
            pltpu.SemaphoreType.DMA((13,)),
            pltpu.SemaphoreType.DMA((13,)),
        ],
        compiler_params=pltpu.CompilerParams(
            collective_id=0, has_side_effects=True, vmem_limit_bytes=62 * 1024 * 1024
        ),
    )(
        jnp.transpose(seg_state[0, 0, 0], (1, 0, 2)),
        seg_cells[0, 0, 0],
        seg_nodes[0, 0, 0],
        pair_blocks[0, 0, 0],
        pair_offsets[0, 0],
        pair_count.reshape(1),
        jnp.asarray(far_table),
        jnp.asarray(fold),
    )
    return out.reshape(1, 1, 1, 3, BLOCKS * WIDTH)


def solution(mesh):
    placed = (
        P("gx", "gy", "gz", None, None, None),
        P("gx", "gy", "gz", None, None),
        P("gx", "gy", "gz", None, None),
        P("gx", "gy", "gz", None, None),
        P("gx", "gy", "gz", None),
        P("gx", "gy", "gz"),
    )
    return jax.shard_map(
        shards,
        mesh=mesh,
        in_specs=placed,
        out_specs=P("gx", "gy", "gz", None, None),
        check_vma=False,
    )
```

time: 67.7 us -> 57.2 us (0.84)
  Pallas kernels: 62.8 us -> 54.9 us
  local copies, waits for them, and re-layouts: 3.9 us -> 1.42 us
    pallas_call x1, Pallas kernels: 62.8 us -> 54.9 us  [shards(): pl.pallas_call(kernel, out_shape=jax.ShapeDtypeStruct((3, BLOCKS, WIDTH),...]
    unnamed x15 -> x1, local copies, waits for them, and re-layouts: 3.81 us -> 1.42 us
where the time goes in v2:
time: 57.2 us; the launch traced here: 57 us
  Pallas kernels  54.9 us (96%)
  local copies, waits for them, and re-layouts  1.42 us (2%)
  between operations  0.66 us (1%)
    pallas_call x1, Pallas kernels, shards(): pl.pallas_call(kernel, out_shape=jax.ShapeDtypeStruct((3, BLOCKS, WIDTH),...  54.9 us
    unnamed x1, local copies, waits for them, and re-layouts  1.42 us

profile of v2, /device:TPU:1, one launch (start us, length us, event | category | flops | bytes accessed | tf_op | source)
XLA Modules:
  0.0 57.0 jit_solution(3675048133766735592)
XLA Ops:
  0.7 54.9 %shard_map.82 = f32[3,32,128]{2,1,0:T(8,128)} custom-call(f32[9,32,128]{2,1,0:T(8,128)} %bitcast.11, s32[32,128]{1,0:T(8,128)} %bitcast.13, s32[2,4096]{1,0:T(2,128)} %bitcast.12, s32[2,128]{1,0:T(2,128)} %bitcast.14, s32[1,128]{1,0:T(1,128)} %bitcast.15, s32[1]{0:T(128)} %bitcast.9.count, bf16[256,768]{1,0:T(8,128)(2,1)} %constant.4.clone.far_in, ...), custom_call_target="tpu_custom_call" | custom-call | tf_op jit(solution)/shard_map/pallas_call | solution.py:606
  55.6 1.4 %copy.13 = f32[1,1,1,3,4096]{4,2,3,1,0:T(1,128)} copy(f32[1,1,1,3,4096]{4,2,3,1,0:T(1,128)} %bitcast.10) | data formatting | bytes 98304

commit v3 on v2

--- a/solution.py
+++ b/solution.py
@@ -18,7 +18,7 @@
 SLOTS = 128
 TILES = 36
 CELL_DEV = 16
-UNROLL = 8
+UNROLL = 16
 SIDES = (-1, 0, 1)
 F32 = jnp.float32
 BF16 = jnp.bfloat16
@@ -53,33 +53,44 @@
 
 
 def block_rows(tile, last, rows):
-    zero = jnp.zeros_like(tile)
-    middle = (rows >= 3) & (rows < 6)
-    line = jnp.where(middle, tile, zero)
-    place = jnp.where(rows < 3, tile, zero)
-    burgers = jnp.where(rows == 5, last, pltpu.roll(tile, 5, 0))
-    burgers = jnp.where(middle, burgers, zero)
-    return line, place, burgers
+    turned = pltpu.roll(tile, 5, 0)
+    line = jnp.where(rows < 3, turned, tile)
+    burgers = jnp.where(rows < 2, pltpu.roll(tile, 2, 0), turned)
+    burgers = jnp.where((rows == 2) | (rows == 5), last, burgers)
+    return line, burgers
+
+
+def outer_rows(first, second, rows):
+    low = jnp.where(rows < 3, first[0:1], first[1:2]) * second
+    low = jnp.where(rows < 6, low, 0.0)
+    high = jnp.where(rows < 3, first[2:3] * second, 0.0)
+    return low, high
+
+
+def dist_rows(place, norm_row, one_row, rows):
+    return jnp.where(rows < 3, place, jnp.where(rows == 3, norm_row, jnp.where(rows == 4, one_row, 0.0)))
 
 
 def prepare_block(i, dom, feats, weights_rows):
     rows = row_ids((8, WIDTH))
     tile = dom[i]
-    tile = tile - jnp.where(rows < 3, 0.5, 0.0)
     last = dom[32 + (i >> 3), pl.ds(i & 7, 1), :]
-    line, place, burgers = block_rows(tile, last, rows)
+    line, burgers = block_rows(tile, last, rows)
+    place = jnp.where(rows < 3, tile - 0.5, 0.0)
     norm = jnp.sum(place * place, axis=0, keepdims=True)
     scale = 1.0 / CORE_SQUARED
-    low = line - 2.0 * scale * place
-    high = burgers + jnp.where(rows == 0, scale, jnp.where(rows == 1, scale * norm + 1.0, 0.0))
-    full = jnp.concatenate([low, high], axis=0)
-    first = head(full)
-    second = head(full - first)
-    third = head(full - first - second)
+    outer = jnp.concatenate(outer_rows(line, burgers, rows), axis=0)
+    outer_1 = head(outer)
+    dist = dist_rows(-2.0 * scale * place, scale, scale * norm + 1.0, rows)
+    first = head(dist)
+    second = head(dist - first)
+    third = head(dist - first - second)
+    gap = jnp.zeros((16, WIDTH), F32)
     stack = jnp.concatenate(
-        [first, first, second, first, second, third, jnp.zeros((32, WIDTH), F32)], axis=0
+        [outer_1, outer_1, outer - outer_1, gap, first, first, first, second, second, third, gap], axis=0
     )
-    feats[i] = jnp.transpose(stack).astype(BF16)
+    turned = jnp.transpose(stack).astype(BF16)
+    feats[i] = turned
     place_first = head(place)
     ones = jnp.where(rows == 3, 1.0, 0.0)
     held = pair16(place_first + ones, place - place_first)
@@ -88,7 +99,6 @@
 
 def pair_group(group, blocks, codes, dom, ghosts, shifts, feats, weights_rows, own_out, peer_out, unroll):
     rows = row_ids((8, WIDTH))
-    zero = jnp.zeros((8, WIDTH), F32)
     centre = jnp.where(rows < 3, 0.5, 0.0)
     ones = jnp.where(rows == 3, 1.0, 0.0)
     loaded = []
@@ -97,48 +107,46 @@
         i = blocks[0, slot]
         g = codes[0, slot]
         j = blocks[1, slot]
-        tile = ghosts[g, j] + shifts[g]
+        tile = ghosts[g, j]
         last = ghosts[g, 32 + (j >> 3), pl.ds(j & 7, 1), :]
-        line, place, burgers = block_rows(tile, last, rows)
+        line, burgers = block_rows(tile, last, rows)
+        place = jnp.where(rows < 3, tile + shifts[g], 0.0)
         norm = jnp.sum(place * place, axis=0, keepdims=True)
-        extra = jnp.where(rows == 0, norm, jnp.where(rows == 1, 1.0, 0.0))
-        line_1 = head(line)
-        line_2 = line - line_1
-        burgers_1 = head(burgers)
-        burgers_2 = burgers - burgers_1
-        place_1 = head(place)
-        place_r = place - place_1
-        place_2 = head(place_r)
-        extra_1 = head(extra)
-        extra_r = extra - extra_1
-        extra_2 = head(extra_r)
-        top = jnp.concatenate(
-            [pair16(line_1, zero), pair16(zero, burgers_1), pair16(burgers_1, zero), pair16(zero, line_1)], axis=1
-        )
-        mid = jnp.concatenate(
-            [pair16(line_2, zero), pair16(zero, burgers_2), pair16(burgers_2, zero), pair16(zero, line_2)], axis=1
-        )
-        products = jnp.concatenate([top, mid, top], axis=0)
-        dist_1 = pair16(place_1, extra_1)
-        dist_2 = pair16(place_2, extra_2)
-        dist_3 = pair16(place_r - place_2, extra_r - extra_2)
-        dists = jnp.concatenate([dist_1, dist_2, dist_1, dist_3, dist_2, dist_1], axis=0)
-        held = pair16(place_1 + ones, place_r)
+        same = jnp.concatenate(outer_rows(line, burgers, rows), axis=0)
+        crossed = jnp.concatenate(outer_rows(burgers, line, rows), axis=0)
+        same_1 = same.astype(BF16)
+        same_2 = (same - same_1.astype(F32)).astype(BF16)
+        crossed_1 = crossed.astype(BF16)
+        crossed_2 = (crossed - crossed_1.astype(F32)).astype(BF16)
+        top = jnp.concatenate([same_1, crossed_1], axis=1)
+        products = jnp.concatenate([top, jnp.concatenate([same_2, crossed_2], axis=1), top], axis=0)
+        dist = dist_rows(place, norm, 1.0, rows)
+        first = head(dist)
+        rest = dist - first
+        second = head(rest)
+        dists = jnp.concatenate(
+            [
+                jnp.zeros((64, WIDTH), BF16),
+                pair16(first, second),
+                pair16(rest - second, first),
+                pair16(second, first),
+                jnp.zeros((16, WIDTH), BF16),
+            ],
+            axis=0,
+        )
+        place_1 = jnp.where(rows < 3, first, 0.0)
+        held = pair16(place_1 + ones, place - place_1)
         held = jnp.concatenate([held, held], axis=1)
         loaded.append((slot, i, place, products, dists, held))
     outs = []
     for slot, i, place, products, dists, held in loaded:
         feat = feats[i]
-        outs.append((dot(feat[:, :48], products), dot(feat[:, :96], dists)))
+        outs.append((dot(feat[:, :48], products), dot(feat, dists)))
     strengths = []
-    for four, dist in outs:
+    for both, dist in outs:
         inv = lax.rsqrt(dist)
         inv_sq = inv * inv
-        line_line = four[:, 0:128]
-        burgers_burgers = four[:, 128:256]
-        line_burgers = four[:, 256:384]
-        burgers_line = four[:, 384:512]
-        strength = (inv_sq * inv) * (line_line * burgers_burgers + (line_burgers * burgers_line) * inv_sq)
+        strength = (inv_sq * inv) * (both[:, 0:128] + both[:, 128:256] * inv_sq)
         high = strength.astype(BF16)
         low = (strength - high.astype(F32)).astype(BF16)
         strengths.append((high, low))
@@ -172,15 +180,16 @@
     rows = row_ids((8, WIDTH))
     tile = dom[b]
     last = dom[32 + (b >> 3), pl.ds(b & 7, 1), :]
-    line, _, burgers = block_rows(tile, last, rows)
+    line, burgers = block_rows(tile, last, rows)
     hot = row_ids((CELL_DEV, WIDTH)) == cells[pl.ds(b, 1), :]
     line_1 = head(line)
     line_2 = line - line_1
+    burgers = jnp.where(rows < 3, burgers, 0.0)
     burgers_1 = head(burgers)
     burgers_2 = burgers - burgers_1
     zero = jnp.zeros((CELL_DEV, WIDTH), F32)
     spread = [
-        jnp.concatenate([jnp.where(hot, part[3 + k : 4 + k], zero) for k in range(3)], axis=0).astype(BF16)
+        jnp.concatenate([jnp.where(hot, part[k : k + 1], zero) for k in range(3)], axis=0).astype(BF16)
         for part in (line_1, line_2)
     ]
     pad = jnp.zeros((8, WIDTH), F32)
@@ -222,7 +231,7 @@
     index = np.arange(CELL_DEV)
     inner = np.stack([index // 4, index // 2 % 2, index % 2])
     rel = np.arange(256)
-    away = np.stack([rel // 64 * 4, (rel // 8 % 8 - 3) * 2, (rel % 8 - 3) * 2])
+    away = np.stack([rel // 64 * 4, (rel // 8 % 8 - 1) * 2, (rel % 8 - 1) * 2])
     delta = away[:, None, None, :] + inner[:, :, None, None] - inner[:, None, :, None]
     delta = (delta + 8) % 16 - 8
     dist = np.sqrt(np.maximum((delta.astype(np.float64) ** 2).sum(0), 1.0))
@@ -363,11 +372,7 @@
         return copy
 
     def spread_of_8(ref_of, at):
-        for distance, moves in (
-            (1, ((3, 4, 1, -1), (3, 2, 1, 1))),
-            (2, ((3, 5, 2, -1), (2, 0, 2, 1))),
-            (2, ((5, 7, 1, -1),)),
-        ):
+        for distance, moves in ((1, ((1, 2, 1, -1), (1, 0, 1, 1))), (3, ((0, 3, 3, -1), (1, 6, 2, 1)))):
             sent = [
                 gather(ref_of(first, count), ref_of(target, count), at(sign * distance))
                 for first, target, count, sign in moves
@@ -381,7 +386,7 @@
             lambda first, count: group_z.at[pl.ds(8 * first, 8 * count)], lambda d: (me_x, me_y, at_z(d))
         )
         for a in range(3):
-            group_xy[0, 3, 8 * a : 8 * a + 8, :] = group_z[pl.ds(3 + a, 8, stride=8), :]
+            group_xy[0, 1, 8 * a : 8 * a + 8, :] = group_z[pl.ds(a, 8, stride=8), :]
         yield from spread_of_8(
             lambda first, count: group_xy.at[0, pl.ds(first, count)], lambda d: (me_x, at_y(d), me_z)
         )
@@ -412,13 +417,14 @@
     moments = lax.fori_loop(
         0, BLOCKS, lambda b, total: moment_block(b, dom, cells, total), jnp.zeros((16, 48), F32), unroll=4
     )
-    group_z[24:32, :] = jnp.concatenate([moments[0:8], jnp.zeros((8, 80), F32)], axis=1)
-    gather_step()
+    group_z[8:16, :] = jnp.concatenate([moments[0:8], jnp.zeros((8, 80), F32)], axis=1)
 
     for part in (0, 1):
         await_ghost(0, 0, OFF, part)
         for e in (-1, 1):
             pass_x(ghost(0, 0, OFF), e, 0, OFF, part)
+    await_ghost(0, 0, ON)
+    gather_step()
     features_part(0)
     for part in (0, 1):
         for dx in (-1, 1):
@@ -426,7 +432,6 @@
             pass_y(ghost(dx, 0, OWN), -dx, dx, OWN, part)
     for dx in (-1, 1):
         pass_on(ghost(dx, 0, OWN), dx, 0)
-    gather_step()
     features_part(1)
     for part in (0, 1):
         for dy in (-1, 1):
@@ -442,7 +447,6 @@
             await_ghost(dx, 0, OFF, part)
             pass_y(ghost(dx, 0, OFF), dx, dx, OFF, part)
     features_part(3)
-    gather_step()
     for part in (0, 1):
         for d in (-1, 1):
             await_ghost(d, d, OWN, part)
@@ -470,7 +474,6 @@
                 )
     loads[2].wait()
     lax.fori_loop(0, BLOCKS, nodes_of, 0, unroll=2)
-    gather_step()
     lines = [raw[3 + k] for k in range(3)]
     length = 0.5 * jnp.sqrt(lines[0] * lines[0] + lines[1] * lines[1] + lines[2] * lines[2])
     values[0] = head(length)
@@ -488,7 +491,8 @@
             await_ghost(d, d, OFF, part)
     for dx in SIDES:
         for dy in SIDES:
-            await_ghost(dx, dy, ON)
+            if (dx, dy) != (0, 0):
+                await_ghost(dx, dy, ON)
 
     def pair_part(first, last):
         def body(group, carry):
@@ -499,6 +503,7 @@
 
         lax.fori_loop(first // UNROLL, last // UNROLL, body, 0)
 
+    gather_step()
     pair_part(0, 64)
     gather_step()
     pair_part(64, SLOTS)
@@ -639,8 +644,8 @@
             pltpu.SemaphoreType.DMA((54,)),
             pltpu.SemaphoreType.DMA((18,)),
             pltpu.SemaphoreType.DMA((18,)),
-            pltpu.SemaphoreType.DMA((13,)),
-            pltpu.SemaphoreType.DMA((13,)),
+            pltpu.SemaphoreType.DMA((11,)),
+            pltpu.SemaphoreType.DMA((11,)),
         ],
         compiler_params=pltpu.CompilerParams(
             collective_id=0, has_side_effects=True, vmem_limit_bytes=62 * 1024 * 1024

time: 57.2 us -> 49.3 us (0.86)
  Pallas kernels: 54.9 us -> 47 us
    pallas_call x1, Pallas kernels: 54.9 us -> 47 us  [shards(): pl.pallas_call(kernel, out_shape=jax.ShapeDtypeStruct((3, BLOCKS, WIDTH),...]
where the time goes in v3:
time: 49.3 us; the launch traced here: 49.1 us
  Pallas kernels  47 us (95%)
  local copies, waits for them, and re-layouts  1.42 us (3%)
  between operations  0.66 us (1%)
    pallas_call x1, Pallas kernels, shards(): pl.pallas_call(kernel, out_shape=jax.ShapeDtypeStruct((3, BLOCKS, WIDTH),...  47 us
    unnamed x1, local copies, waits for them, and re-layouts  1.42 us

profile of v3, /device:TPU:1, one launch (start us, length us, event | category | flops | bytes accessed | tf_op | source)
XLA Modules:
  0.0 49.1 jit_solution(2034089890992268911)
XLA Ops:
  0.7 47.0 %shard_map.82 = f32[3,32,128]{2,1,0:T(8,128)} custom-call(f32[9,32,128]{2,1,0:T(8,128)} %bitcast.11, s32[32,128]{1,0:T(8,128)} %bitcast.13, s32[2,4096]{1,0:T(2,128)} %bitcast.12, s32[2,128]{1,0:T(2,128)} %bitcast.14, s32[1,128]{1,0:T(1,128)} %bitcast.15, s32[1]{0:T(128)} %bitcast.9.count, bf16[256,768]{1,0:T(8,128)(2,1)} %constant.4.clone.far_in, ...), custom_call_target="tpu_custom_call" | custom-call | tf_op jit(solution)/shard_map/pallas_call | solution.py:611
  47.7 1.4 %copy.13 = f32[1,1,1,3,4096]{4,2,3,1,0:T(1,128)} copy(f32[1,1,1,3,4096]{4,2,3,1,0:T(1,128)} %bitcast.10) | data formatting | bytes 98304

commit v4 on v3

--- a/solution.py
+++ b/solution.py
@@ -18,7 +18,9 @@
 SLOTS = 128
 TILES = 36
 CELL_DEV = 16
-UNROLL = 16
+UNROLL = 64
+LAG1, LAG2, LAG3 = (2, 4, 4)
+TOGETHER = 16
 SIDES = (-1, 0, 1)
 F32 = jnp.float32
 BF16 = jnp.bfloat16
@@ -79,18 +81,19 @@
     place = jnp.where(rows < 3, tile - 0.5, 0.0)
     norm = jnp.sum(place * place, axis=0, keepdims=True)
     scale = 1.0 / CORE_SQUARED
-    outer = jnp.concatenate(outer_rows(line, burgers, rows), axis=0)
-    outer_1 = head(outer)
+    same = jnp.concatenate(outer_rows(line, burgers, rows), axis=0)
+    same_1 = head(same)
+    crossed = jnp.concatenate(outer_rows(burgers, line, rows), axis=0)
+    crossed_1 = head(crossed)
     dist = dist_rows(-2.0 * scale * place, scale, scale * norm + 1.0, rows)
     first = head(dist)
     second = head(dist - first)
     third = head(dist - first - second)
     gap = jnp.zeros((16, WIDTH), F32)
-    stack = jnp.concatenate(
-        [outer_1, outer_1, outer - outer_1, gap, first, first, first, second, second, third, gap], axis=0
-    )
-    turned = jnp.transpose(stack).astype(BF16)
-    feats[i] = turned
+    stack = jnp.concatenate([same_1, same_1, same - same_1, gap, first, first, first, second, second, third, gap], axis=0)
+    feats[i, 0:WIDTH] = jnp.transpose(stack).astype(BF16)
+    stack = jnp.concatenate([crossed_1, crossed_1, crossed - crossed_1, jnp.zeros((80, WIDTH), F32)], axis=0)
+    feats[i, WIDTH : 2 * WIDTH] = jnp.transpose(stack).astype(BF16)
     place_first = head(place)
     ones = jnp.where(rows == 3, 1.0, 0.0)
     held = pair16(place_first + ones, place - place_first)
@@ -100,9 +103,7 @@
 def pair_group(group, blocks, codes, dom, ghosts, shifts, feats, weights_rows, own_out, peer_out, unroll):
     rows = row_ids((8, WIDTH))
     centre = jnp.where(rows < 3, 0.5, 0.0)
-    ones = jnp.where(rows == 3, 1.0, 0.0)
-    loaded = []
-    for u in range(unroll):
+    def load(u):
         slot = group * unroll + u
         i = blocks[0, slot]
         g = codes[0, slot]
@@ -112,14 +113,10 @@
         line, burgers = block_rows(tile, last, rows)
         place = jnp.where(rows < 3, tile + shifts[g], 0.0)
         norm = jnp.sum(place * place, axis=0, keepdims=True)
-        same = jnp.concatenate(outer_rows(line, burgers, rows), axis=0)
-        crossed = jnp.concatenate(outer_rows(burgers, line, rows), axis=0)
-        same_1 = same.astype(BF16)
-        same_2 = (same - same_1.astype(F32)).astype(BF16)
-        crossed_1 = crossed.astype(BF16)
-        crossed_2 = (crossed - crossed_1.astype(F32)).astype(BF16)
-        top = jnp.concatenate([same_1, crossed_1], axis=1)
-        products = jnp.concatenate([top, jnp.concatenate([same_2, crossed_2], axis=1), top], axis=0)
+        product = jnp.concatenate(outer_rows(line, burgers, rows), axis=0)
+        product_1 = product.astype(BF16)
+        product_2 = (product - product_1.astype(F32)).astype(BF16)
+        products = jnp.concatenate([product_1, product_2, product_1], axis=0)
         dist = dist_rows(place, norm, 1.0, rows)
         first = head(dist)
         rest = dist - first
@@ -134,30 +131,41 @@
             ],
             axis=0,
         )
-        place_1 = jnp.where(rows < 3, first, 0.0)
-        held = pair16(place_1 + ones, place - place_1)
-        held = jnp.concatenate([held, held], axis=1)
-        loaded.append((slot, i, place, products, dists, held))
-    outs = []
-    for slot, i, place, products, dists, held in loaded:
-        feat = feats[i]
-        outs.append((dot(feat[:, :48], products), dot(feat, dists)))
-    strengths = []
-    for both, dist in outs:
+        held = pair16(first, second)
+        return slot, i, place, products, dists, held
+
+    def multiply(slot, i, place, products, dists, held):
+        return dot(feats[i][:, :48], products), dot(feats[i, 0:WIDTH], dists)
+
+    def strength_of(both, dist):
         inv = lax.rsqrt(dist)
         inv_sq = inv * inv
-        strength = (inv_sq * inv) * (both[:, 0:128] + both[:, 128:256] * inv_sq)
+        strength = (inv_sq * inv) * (both[0:128] + both[128:256] * inv_sq)
         high = strength.astype(BF16)
-        low = (strength - high.astype(F32)).astype(BF16)
-        strengths.append((high, low))
-    for (slot, i, place, products, dists, held), (high, low) in zip(loaded, strengths):
+        return high, (strength - high.astype(F32)).astype(BF16)
+
+    def reduce(slot, i, place, products, dists, held, high, low):
         peer = dot(weights_rows[i], jnp.concatenate([high, low], axis=0))
-        own = dot_nt(held, jnp.concatenate([high, low], axis=1))
+        own = dot_nt(jnp.concatenate([held, held], axis=1), jnp.concatenate([high, low], axis=1))
         peer = peer[0:8] + peer[8:16]
         own = own[0:8] + own[8:16]
         home = dom[i] - centre
-        own_out[slot] = home * own[3:4] - own
+        own_out[slot] = home * own[4:5] - own
         peer_out[slot] = place * peer[3:4] - peer
+
+    loaded, outs, strengths = {}, {}, {}
+    for turn in range(unroll + LAG1 + LAG2 + LAG3):
+        if turn < unroll:
+            loaded[turn] = load(turn)
+        u = turn - LAG1
+        if 0 <= u < unroll:
+            outs[u] = multiply(*loaded[u])
+        u -= LAG2
+        if 0 <= u < unroll:
+            strengths[u] = strength_of(*outs.pop(u))
+        u -= LAG3
+        if 0 <= u < unroll:
+            reduce(*loaded.pop(u), *strengths.pop(u))
 
 
 def slot_table(slot_out, live):
@@ -198,31 +206,34 @@
     return total + dot_nt(left, right)
 
 
-def nodes_row(nodes, e, b):
-    return nodes[e : e + 1, pl.ds(pl.multiple_of(b * WIDTH, WIDTH), WIDTH)]
-
-
-def node_onehot(b, nodes, node_hot):
-    lows = [
-        jnp.where(row_ids((128, WIDTH)) == (nodes_row(nodes, e, b) & 127), 1.0, 0.0).astype(BF16)
-        for e in range(2)
-    ]
-    node_hot[b] = jnp.concatenate(lows, axis=1)
-
-
-def node_sums(nodes, node_hot, values, count):
-    together = 4
+def node_tables(nodes, node_rows, node_hot):
+    def copy_row(b, carry):
+        for e in range(2):
+            node_rows[e, pl.ds(b, 1), :] = nodes[e : e + 1, pl.ds(pl.multiple_of(b * WIDTH, WIDTH), WIDTH)]
+        return carry
+
+    lax.fori_loop(0, BLOCKS, copy_row, 0, unroll=4)
+    lanes = lax.broadcasted_iota(jnp.int32, (WIDTH, WIDTH), 1).astype(F32)
+    for e in range(2):
+        lows = (node_rows[e] & 127).astype(F32)
+        turned = jnp.transpose(jnp.concatenate([lows, jnp.zeros((96, WIDTH), F32)], axis=0))
+        for b in range(BLOCKS):
+            node_hot[b, e * WIDTH : (e + 1) * WIDTH, :] = jnp.where(turned[:, b : b + 1] == lanes, 1.0, 0.0).astype(BF16)
+
+
+def node_sums(node_rows, node_hot, values, count):
+    together = TOGETHER
 
     def body(turn, total):
         parts, hots = [], []
         for u in range(together):
             b = turn * together + u
             for e in range(2):
-                hit = row_ids((32, WIDTH)) == nodes_row(nodes, e, b) >> 7
+                hit = row_ids((32, WIDTH)) == node_rows[e, pl.ds(b, 1), :] >> 7
                 rows = [jnp.where(hit, values[c, pl.ds(b, 1), :], 0.0) for c in range(2 * count)]
                 parts.append(jnp.concatenate(rows, axis=0).astype(BF16))
             hots.append(node_hot[b])
-        return total + dot_nt(jnp.concatenate(parts, axis=1), jnp.concatenate(hots, axis=1))
+        return total + dot(jnp.concatenate(parts, axis=1), jnp.concatenate(hots, axis=0))
 
     return lax.fori_loop(0, BLOCKS // together, body, jnp.zeros((64 * count, WIDTH), F32))
 
@@ -253,7 +264,7 @@
     state_in, cells_in, nodes_in, blocks_in, codes_in, count, far_in, fold_in, out,
     raw, cells, nodes, block_ids, code_ids, blocks, codes, far_table, fold,
     dom, ghosts, shifts, feats, weights_rows, own_out, peer_out, react, from_on, from_off, from_layer,
-    node_hot, node_len, values, group_z, group_xy,
+    node_rows, node_hot, node_len, values, group_z, group_xy,
     load_sem, halo_send, halo_recv, react_send, react_recv, gather_send, gather_recv,
 ):
     size_x, size_y, size_z = 4, 8, 8
@@ -408,10 +419,6 @@
 
     def features_part(number):
         lax.fori_loop(4 * number, 4 * number + 4, features, 0, unroll=2)
-
-    def nodes_of(b, carry):
-        node_onehot(b, nodes, node_hot)
-        return carry
 
     loads[1].wait()
     moments = lax.fori_loop(
@@ -473,12 +480,12 @@
                     jnp.where(rows == 1, dy - 0.5, jnp.where(rows == 2, dz - 0.5, 0.0)),
                 )
     loads[2].wait()
-    lax.fori_loop(0, BLOCKS, nodes_of, 0, unroll=2)
+    node_tables(nodes, node_rows, node_hot)
     lines = [raw[3 + k] for k in range(3)]
     length = 0.5 * jnp.sqrt(lines[0] * lines[0] + lines[1] * lines[1] + lines[2] * lines[2])
     values[0] = head(length)
     values[1] = length - head(length)
-    sums = node_sums(nodes, node_hot, values, 1)
+    sums = node_sums(node_rows, node_hot, values, 1)
     node_len[...] = jnp.maximum(sums[0:32] + sums[32:64], DRAG_FLOOR)
     for load in loads[3:]:
         load.wait()
@@ -597,7 +604,7 @@
         half = 0.5 * (force[c] + near[:, 128 * c : 128 * c + 128])
         values[c] = head(half)
         values[3 + c] = half - head(half)
-    sums = node_sums(nodes, node_hot, values, 3)
+    sums = node_sums(node_rows, node_hot, values, 3)
     for c in range(3):
         out[c] = (sums[32 * c : 32 * c + 32] + sums[96 + 32 * c : 128 + 32 * c]) / node_len[...]
 
@@ -626,7 +633,7 @@
             pltpu.VMEM((TILES, 8, WIDTH), F32),
             pltpu.VMEM((27, TILES, 8, WIDTH), F32),
             pltpu.VMEM((27, 8, WIDTH), F32),
-            pltpu.VMEM((BLOCKS, 128, WIDTH), BF16),
+            pltpu.VMEM((BLOCKS, 256, WIDTH), BF16),
             pltpu.VMEM((BLOCKS, 16, 256), BF16),
             pltpu.VMEM((SLOTS, 8, WIDTH), F32),
             pltpu.VMEM((SLOTS, 8, WIDTH), F32),
@@ -634,7 +641,8 @@
             pltpu.VMEM((288, 384), F32),
             pltpu.VMEM((288, 384), F32),
             pltpu.VMEM((8, 32, 384), F32),
-            pltpu.VMEM((BLOCKS, 128, 256), BF16),
+            pltpu.VMEM((2, BLOCKS, WIDTH), jnp.int32),
+            pltpu.VMEM((BLOCKS, 256, WIDTH), BF16),
             pltpu.VMEM((32, WIDTH), F32),
             pltpu.VMEM((6, BLOCKS, WIDTH), F32),
             pltpu.VMEM((64, WIDTH), F32),

time: 49.3 us -> 47 us (0.953)
  Pallas kernels: 47 us -> 44.6 us
    pallas_call x1, Pallas kernels: 47 us -> 44.6 us  [shards(): pl.pallas_call(kernel, out_shape=jax.ShapeDtypeStruct((3, BLOCKS, WIDTH),...]
where the time goes in v4:
time: 47 us; the launch traced here: 46.7 us
  Pallas kernels  44.6 us (95%)
  local copies, waits for them, and re-layouts  1.42 us (3%)
  between operations  0.66 us (1%)
    pallas_call x1, Pallas kernels, shards(): pl.pallas_call(kernel, out_shape=jax.ShapeDtypeStruct((3, BLOCKS, WIDTH),...  44.6 us
    unnamed x1, local copies, waits for them, and re-layouts  1.42 us

profile of v4, /device:TPU:1, one launch (start us, length us, event | category | flops | bytes accessed | tf_op | source)
XLA Modules:
  0.0 46.7 jit_solution(10679734502552110347)
XLA Ops:
  0.7 44.6 %shard_map.82 = f32[3,32,128]{2,1,0:T(8,128)} custom-call(f32[9,32,128]{2,1,0:T(8,128)} %bitcast.11, s32[32,128]{1,0:T(8,128)} %bitcast.13, s32[2,4096]{1,0:T(2,128)} %bitcast.12, s32[2,128]{1,0:T(2,128)} %bitcast.14, s32[1,128]{1,0:T(1,128)} %bitcast.15, s32[1]{0:T(128)} %bitcast.9.count, bf16[256,768]{1,0:T(8,128)(2,1)} %constant.4.clone.far_in, ...), custom_call_target="tpu_custom_call" | custom-call | tf_op jit(solution)/shard_map/pallas_call | solution.py:618
  45.3 1.4 %copy.13 = f32[1,1,1,3,4096]{4,2,3,1,0:T(1,128)} copy(f32[1,1,1,3,4096]{4,2,3,1,0:T(1,128)} %bitcast.10) | data formatting | bytes 98304

commit v5 on v4

--- a/solution.py
+++ b/solution.py
@@ -1,6 +1,5 @@
 import jax
 import jax.numpy as jnp
-import ml_dtypes
 import numpy as np
 from jax import lax
 from jax.experimental import pallas as pl
@@ -19,8 +18,8 @@
 TILES = 36
 CELL_DEV = 16
 UNROLL = 64
-LAG1, LAG2, LAG3 = (2, 4, 4)
-TOGETHER = 16
+LAG1, LAG2, LAG3 = (3, 4, 5)
+TOGETHER = 32
 SIDES = (-1, 0, 1)
 F32 = jnp.float32
 BF16 = jnp.bfloat16
@@ -247,17 +246,12 @@
     delta = (delta + 8) % 16 - 8
     dist = np.sqrt(np.maximum((delta.astype(np.float64) ** 2).sum(0), 1.0))
     far = np.where(np.abs(delta).max(0) > 1, FAR_STRENGTH / dist, 0.0).astype(np.float32)
-    far = far.reshape(256, 256)
-    first = far.astype(ml_dtypes.bfloat16)
-    second = (far - first.astype(np.float32)).astype(ml_dtypes.bfloat16)
-    table = np.concatenate([first, first, second], axis=1)
     lanes = np.arange(384)
     part = lanes % 128
     fold = np.zeros((16, 384), np.float32)
     for lane in lanes[part < 48]:
         fold[3 * (lane // 128) + part[lane] // 16, lane] = 1.0
-    fold = np.concatenate([fold, fold], axis=1).astype(ml_dtypes.bfloat16)
-    return table, fold
+    return far.reshape(256, 256), fold
 
 
 def kernel(
@@ -460,12 +454,12 @@
             pass_off(ghost(d, d, OWN), d, d, part)
     for d in (-1, 1):
         pass_on(ghost(d, d, OWN), d, d)
+    gather_step()
     features_part(4)
     for d in (-1, 1):
         for part in (0, 1):
             await_ghost(d, -d, OWN, part)
         pass_on(ghost(d, -d, OWN), d, -d)
-    gather_step()
     for number in range(5, 8):
         features_part(number)
 
@@ -566,7 +560,10 @@
         first = held.astype(BF16)
         second = (held - first.astype(F32)).astype(BF16)
         sides.append(jnp.concatenate([first, second, first], axis=0))
-    spread = dot(far_table[...], jnp.concatenate(sides, axis=1))
+    far = far_table[...]
+    first = far.astype(BF16)
+    second = (far - first.astype(F32)).astype(BF16)
+    spread = dot(jnp.concatenate([first, first, second], axis=1), jnp.concatenate(sides, axis=1))
     source = lax.broadcasted_iota(jnp.int32, (256, 384), 0) >> 4
     lane = lax.broadcasted_iota(jnp.int32, (256, 384), 1) & 15
     spread = jnp.where(source == lane, spread, 0.0)
@@ -576,7 +573,8 @@
     folded = jnp.concatenate([folded, jnp.zeros((112, 384), F32)], axis=0)
     first = folded.astype(BF16)
     second = (folded - first.astype(F32)).astype(BF16)
-    field = dot_nt(fold[...], jnp.concatenate([first, second], axis=1))
+    folds = fold[...].astype(BF16)
+    field = dot_nt(jnp.concatenate([folds, folds], axis=1), jnp.concatenate([first, second], axis=1))
     cell = cells[...]
     hits = [cell == m for m in range(CELL_DEV)]
     per_seg = []
@@ -628,8 +626,8 @@
             pltpu.VMEM((1, SLOTS), jnp.int32),
             pltpu.SMEM((2, SLOTS), jnp.int32),
             pltpu.SMEM((1, SLOTS), jnp.int32),
-            pltpu.VMEM(far_table.shape, BF16),
-            pltpu.VMEM(fold.shape, BF16),
+            pltpu.VMEM(far_table.shape, F32),
+            pltpu.VMEM(fold.shape, F32),
             pltpu.VMEM((TILES, 8, WIDTH), F32),
             pltpu.VMEM((27, TILES, 8, WIDTH), F32),
             pltpu.VMEM((27, 8, WIDTH), F32),

time: 47 us -> 46.3 us (0.985)
  Pallas kernels: 44.6 us -> 44 us
    pallas_call x1, Pallas kernels: 44.6 us -> 44 us  [shards(): pl.pallas_call(kernel, out_shape=jax.ShapeDtypeStruct((3, BLOCKS, WIDTH),...]
where the time goes in v5:
time: 46.3 us; the launch traced here: 46.1 us
  Pallas kernels  44 us (95%)
  local copies, waits for them, and re-layouts  1.42 us (3%)
  between operations  0.66 us (1%)
    pallas_call x1, Pallas kernels, shards(): pl.pallas_call(kernel, out_shape=jax.ShapeDtypeStruct((3, BLOCKS, WIDTH),...  44 us
    unnamed x1, local copies, waits for them, and re-layouts  1.42 us

profile of v5, /device:TPU:1, one launch (start us, length us, event | category | flops | bytes accessed | tf_op | source)
XLA Modules:
  0.0 46.1 jit_solution(12523679399203880595)
XLA Ops:
  0.7 44.0 %shard_map.82 = f32[3,32,128]{2,1,0:T(8,128)} custom-call(f32[9,32,128]{2,1,0:T(8,128)} %bitcast.11, s32[32,128]{1,0:T(8,128)} %bitcast.13, s32[2,4096]{1,0:T(2,128)} %bitcast.12, s32[2,128]{1,0:T(2,128)} %bitcast.14, s32[1,128]{1,0:T(1,128)} %bitcast.15, s32[1]{0:T(128)} %bitcast.9.count, f32[256,256]{1,0:T(8,128)} %constant.4.clone.far_in, ...), custom_call_target="tpu_custom_call" | custom-call | tf_op jit(solution)/shard_map/pallas_call | solution.py:616
  44.7 1.4 %copy.13 = f32[1,1,1,3,4096]{4,2,3,1,0:T(1,128)} copy(f32[1,1,1,3,4096]{4,2,3,1,0:T(1,128)} %bitcast.10) | data formatting | bytes 98304

commit v6 on v5

--- a/solution.py
+++ b/solution.py
@@ -592,12 +592,12 @@
         pulled[0] * lines[1] - pulled[1] * lines[0],
     ]
 
-    for copy in reacts[1:]:
-        copy.wait_recv()
+    for d in range(9):
+        reacts[1 + d].wait_recv()
+        near = near + from_off[pl.ds(32 * d, 32), :]
     for number in range(8):
+        reacts[10 + number].wait_recv()
         near = near + from_layer[number]
-    for d in range(9):
-        near = near + from_off[pl.ds(32 * d, 32), :]
     for c in range(3):
         half = 0.5 * (force[c] + near[:, 128 * c : 128 * c + 128])
         values[c] = head(half)

time: 46.3 us -> 46.3 us (level)
  no operation moved by 1% of the time
where the time goes in v6:
time: 46.3 us; the launch traced here: 46.1 us
  Pallas kernels  44 us (95%)
  local copies, waits for them, and re-layouts  1.42 us (3%)
  between operations  0.66 us (1%)
    pallas_call x1, Pallas kernels, shards(): pl.pallas_call(kernel, out_shape=jax.ShapeDtypeStruct((3, BLOCKS, WIDTH),...  44 us
    unnamed x1, local copies, waits for them, and re-layouts  1.42 us

profile of v6, /device:TPU:1, one launch (start us, length us, event | category | flops | bytes accessed | tf_op | source)
XLA Modules:
  0.0 46.1 jit_solution(14378157047805795692)
XLA Ops:
  0.7 44.0 %shard_map.82 = f32[3,32,128]{2,1,0:T(8,128)} custom-call(f32[9,32,128]{2,1,0:T(8,128)} %bitcast.11, s32[32,128]{1,0:T(8,128)} %bitcast.13, s32[2,4096]{1,0:T(2,128)} %bitcast.12, s32[2,128]{1,0:T(2,128)} %bitcast.14, s32[1,128]{1,0:T(1,128)} %bitcast.15, s32[1]{0:T(128)} %bitcast.9.count, f32[256,256]{1,0:T(8,128)} %constant.4.clone.far_in, ...), custom_call_target="tpu_custom_call" | custom-call | tf_op jit(solution)/shard_map/pallas_call | solution.py:616
  44.7 1.4 %copy.13 = f32[1,1,1,3,4096]{4,2,3,1,0:T(1,128)} copy(f32[1,1,1,3,4096]{4,2,3,1,0:T(1,128)} %bitcast.10) | data formatting | bytes 98304
